TPU v7x, 256 devices: a whole 4x4x8 slice. The times are simulated.
256 devices in a mesh: ctx: 16 (over x, y_hi, core), tp: 16 (over y_lo, z).
Axes of the slice: x: 4, y: 4 (y_hi: 2, y_lo: 2; y = y_hi * 2 + y_lo), z: 8, core: 2. Of those that a mesh axis runs over, the one named last changes fastest.
Arguments:
- queries: bfloat16 [8192, 8192], P('ctx', 'tp'), may hold values from -6 to 6
- keys: bfloat16 [8192, 8192], P('ctx', 'tp'), may hold values from -6 to 6
- values: bfloat16 [8192, 8192], P('ctx', 'tp'), may hold values from -6 to 6
- positions: int32 [8192], P('ctx'), may hold values from 0 to 2047, as said below
- lambda_query: float32 [32, 256], P('tp'), may hold values from -0.6 to 0.6
- lambda_key: float32 [32, 256], P('tp'), may hold values from -0.6 to 0.6
- norm_gain: float32 [256], replicated, may hold values from 0.25 to 1.75
- out_weight: bfloat16 [8192, 8192], P('tp'), may hold values from -0.0625 to 0.0625
Outputs:
- mixed: bfloat16 [8192, 8192], P(('ctx', 'tp'))
Inputs may be any that keep to these rules, and one draw needn't show every extreme that they name: positions[j] counts token j's place in its document: 0 at a document's first token, rising by one per token. The batch holds 8 documents of 2 to 2048 tokens each, one of exactly 2048 tokens.
All inputs are finite; a program needn't handle non-finite values.
Results may differ from a plain program's by a relative error of at most 0.0059.
Values may be sent and summed in bfloat16 or wider, within the bound.
No kernel may reach another device: no remote copies, remote signals or barrier semaphores. Data moves between devices by JAX's collectives and lax.ppermute only.
A program may use at most 128 MiB of HBM per device.

v0:
```python
import math

import jax
import jax.numpy as jnp
from jax import lax
from jax.sharding import PartitionSpec as P

NEG = -1e30
EPS = 1e-05
LAMBDA_INIT = 0.8 - 0.6 * math.exp(-3.3)


def shifted(value, axis, steps):
    count = lax.axis_size(axis)
    first, last = (max(0, -steps), min(count, count - steps))
    return lax.ppermute(value, axis, [(source, source + steps) for source in range(first, last)])


def shards(queries, keys, values, positions, lambda_query, lambda_key, norm_gain, out_weight):
    row_count = queries.shape[0]
    head_count = lambda_query.shape[0]
    head_width = lambda_query.shape[1]
    half_width = head_width // 2
    reach_blocks = (row_count * lax.axis_size("ctx") // 4 + row_count - 2) // row_count
    anchor = lax.axis_index("ctx") * row_count
    query_pos = anchor + jnp.arange(row_count, dtype=jnp.int32)
    doc_start = query_pos - positions
    lambda_head = (
        jnp.exp(jnp.sum(lambda_query[:, :half_width] * lambda_key[:, :half_width], axis=1))
        - jnp.exp(jnp.sum(lambda_query[:, half_width:] * lambda_key[:, half_width:], axis=1))
        + LAMBDA_INIT
    )
    blocks = [(keys, values)]
    for offset in range(1, reach_blocks + 1):
        blocks.append(shifted((keys, values), "ctx", offset))
    query_four = queries.reshape(row_count, head_count, 2, half_width)
    score_scale = half_width ** (-0.5)
    masks = []
    score_list = []
    for offset in range(len(blocks)):
        key_pos = anchor - offset * row_count + jnp.arange(row_count, dtype=jnp.int32)
        live = (key_pos[None, :] >= doc_start[:, None]) & (key_pos[None, :] <= query_pos[:, None])
        key_four = blocks[offset][0].reshape(row_count, head_count, 2, half_width)

        def make_scores(key_four=key_four, live=live):
            raw = (
                jnp.einsum(
                    "qhmd,khmd->hmqk", query_four, key_four, preferred_element_type=jnp.float32
                )
                * score_scale
            )
            return jnp.where(live[None, None], raw, NEG)

        scores = make_scores()
        masks.append(live)
        score_list.append(scores)
    row_max = score_list[0].max(axis=-1)
    for scores in score_list[1:]:
        row_max = jnp.maximum(row_max, scores.max(axis=-1))
    totals = jnp.zeros((head_count, 2, row_count), jnp.float32)
    summed = jnp.zeros((row_count, head_count, 2, head_width), jnp.float32)
    for offset in range(len(blocks)):
        live = masks[offset]
        weights = jnp.where(live[None, None], jnp.exp(score_list[offset] - row_max[..., None]), 0.0)
        totals = totals + jnp.sum(weights, axis=-1)
        rounded = weights.astype(jnp.bfloat16)
        value_three = blocks[offset][1].reshape(row_count, head_count, head_width)

        def make_product(rounded=rounded, value_three=value_three):
            return jnp.einsum(
                "hmqk,khe->qhme", rounded, value_three, preferred_element_type=jnp.float32
            )

        summed = summed + make_product()
    total_first = jnp.transpose(totals[:, 0, :])[:, :, None]
    total_second = jnp.transpose(totals[:, 1, :])[:, :, None]
    combined = (
        summed[:, :, 0] / total_first - lambda_head[None, :, None] * summed[:, :, 1] / total_second
    )
    normed = combined * lax.rsqrt(jnp.mean(combined * combined, axis=-1, keepdims=True) + EPS)
    attended = (
        (normed * norm_gain * (1.0 - LAMBDA_INIT))
        .astype(jnp.bfloat16)
        .reshape(row_count, head_count * head_width)
    )
    mixed = lax.psum_scatter(
        jnp.dot(attended, out_weight, preferred_element_type=jnp.float32),
        "tp",
        scatter_dimension=0,
        tiled=True,
    )
    return mixed.astype(jnp.bfloat16)


def solution(mesh):
    return jax.shard_map(
        shards,
        mesh=mesh,
        in_specs=(
            P("ctx", "tp"),
            P("ctx", "tp"),
            P("ctx", "tp"),
            P("ctx"),
            P("tp", None),
            P("tp", None),
            P(),
            P("tp", None),
        ),
        out_specs=P(("ctx", "tp"), None),
        check_vma=False,
    )
```

profile of v0, /device:TPU:58, one launch (start us, length us, event | category | flops | bytes accessed | tf_op | source)
XLA Modules:
  0.0 302.4 jit_solution(2522310100439240647)
XLA Ops:
  7.8 3.4 %collective-permute-start.3 = (bf16[512,512]{0,1:T(8,128)(2,1)S(1)}, bf16[512,512]{0,1:T(8,128)(2,1)}, u32[]{:S(2)}, u32[]{:S(2)}) collective-permute-start(bf16[512,512]{0,1:T(8,128)(2,1)S(1)} %copy.53), channel_id=1, source_target_pairs={{0,64},{16,80},{32,96},{48,112},{64,128},{80,144},{96,160},{112,17... | collective-permute-start | bytes 1572872 | tf_op jit(solution)/shard_map/ppermute | solution.py:16
  11.2 2.9 collective-permute-start.2
  14.2 4.2 %collective-permute-start.1 = (bf16[512,512]{0,1:T(8,128)(2,1)S(1)}, bf16[512,512]{0,1:T(8,128)(2,1)}, u32[]{:S(2)}, u32[]{:S(2)}) collective-permute-start(bf16[512,512]{0,1:T(8,128)(2,1)S(1)} %copy.53), channel_id=1, source_target_pairs={{0,32},{16,48},{32,64},{48,80},{64,96},{80,112},{96,128},{112,144}... | collective-permute-start | bytes 1572872 | tf_op jit(solution)/shard_map/ppermute | solution.py:16
  18.4 1.9 collective-permute-start
  20.3 2.9 collective-permute-start.4
  24.4 2.0 copy.90
  30.8 3.7 %collective-permute-start.5 = (bf16[512,512]{1,0:T(8,128)(2,1)}, bf16[512,512]{1,0:T(8,128)(2,1)}, u32[]{:S(2)}, u32[]{:S(2)}) collective-permute-start(bf16[512,512]{1,0:T(8,128)(2,1)} %param.10), channel_id=1, source_target_pairs={{0,32},{16,48},{32,64},{48,80},{64,96},{80,112},{96,128},{112,144}... | collective-permute-start | bytes 1572872 | tf_op jit(solution)/shard_map/ppermute | solution.py:16
  34.5 2.0 fusion.4
  36.6 4.5 %collective-permute-start.6 = (bf16[512,512]{1,0:T(8,128)(2,1)}, bf16[512,512]{1,0:T(8,128)(2,1)}, u32[]{:S(2)}, u32[]{:S(2)}) collective-permute-start(bf16[512,512]{1,0:T(8,128)(2,1)} %param.10), channel_id=1, source_target_pairs={{0,48},{16,64},{32,80},{48,96},{64,112},{80,128},{96,144},{112,160... | collective-permute-start | bytes 1572872 | tf_op jit(solution)/shard_map/ppermute | solution.py:16
  41.1 2.0 fusion.3
  43.2 2.9 collective-permute-done.1
  46.0 3.1 %collective-permute-start.7 = (bf16[512,512]{1,0:T(8,128)(2,1)}, bf16[512,512]{1,0:T(8,128)(2,1)}, u32[]{:S(2)}, u32[]{:S(2)}) collective-permute-start(bf16[512,512]{1,0:T(8,128)(2,1)} %param.10), channel_id=1, source_target_pairs={{0,64},{16,80},{32,96},{48,112},{64,128},{80,144},{96,160},{112,17... | collective-permute-start | bytes 1572872 | tf_op jit(solution)/shard_map/ppermute | solution.py:16
  49.1 2.0 fusion.2
  51.2 2.4 fusion.1
  53.7 5.4 %fusion.7 = (f32[2,2,512]{2,1,0:T(2,128)S(1)}, f32[2,2,512]{2,1,0:T(2,128)S(1)}, f32[2,2,512]{2,1,0:T(2,128)S(1)}, f32[2,2,512]{2,1,0:T(2,128)S(1)}, f32[2,2,512]{2,1,0:T(2,128)S(1)}) fusion(f32[2,2,512,512]{2,3,1,0:T(8,128)S(1)} %get-tuple-element.30, f32[2,2,512]{2,1,0:T(2,128)S(1)} %maximum_maximum_fusion, pred[512,512]{0,1:T(8,128)(4,1)S(1)} %get-tuple-element.16, ...), kind=kLoop, calls=%fused_computation.17 | loop fusion | flops 26204160 | bytes 22331392 | tf_op jit(solution)/shard_map/reduce_sum | solution.py:65
  60.2 4.0 %fusion.21 = f32[2,2,512,256]{2,3,1,0:T(8,128)S(1)} fusion(bf16[512,2,256,1]{0,2,3,1:T(8,128)(2,1)} %bitcast.113, f32[2,2,512,512]{2,3,1,0:T(8,128)} %copy-done.7, f32[2,2,512]{2,1,0:T(2,128)S(1)} %maximum_maximum_fusion, pred[512,512]{0,1:T(8,128)(4,1)S(1)} %get-tuple-element.16), kind=kOutput, calls=%fused_computation.28 | convolution fusion | flops 542113792 | bytes 7086080 | tf_op jit(solution)/shard_map/hmqk,khe->qhme/dot_general | solution.py:70
  64.2 3.0 %fusion.23 = f32[2,2,512,256]{2,3,1,0:T(8,128)} fusion(bf16[512,2,256,1]{0,2,3,1:T(8,128)(2,1)S(1)} %bitcast.112, f32[2,2,512,512]{2,3,1,0:T(8,128)S(1)} %copy-done.5, f32[2,2,512]{2,1,0:T(2,128)S(1)} %maximum_maximum_fusion, pred[512,512]{0,1:T(8,128)(4,1)S(1)} %get-tuple-element.19), kind=kOutput, calls=%fused_computation.29 | convolution fusion | flops 542113792 | bytes 7086080 | tf_op jit(solution)/shard_map/hmqk,khe->qhme/dot_general | solution.py:70
  68.5 5.0 %fusion.19 = f32[2,2,512,256]{2,3,1,0:T(8,128)} fusion(bf16[512,2,256,1]{0,2,3,1:T(8,128)(2,1)S(1)} %bitcast.114, f32[2,2,512,512]{2,3,1,0:T(8,128)} %copy-done.6, f32[2,2,512]{2,1,0:T(2,128)S(1)} %maximum_maximum_fusion, pred[512,512]{0,1:T(8,128)(4,1)S(1)} %get-tuple-element.20), kind=kOutput, calls=%fused_computation.27 | convolution fusion | flops 542113792 | bytes 7086080 | tf_op jit(solution)/shard_map/hmqk,khe->qhme/dot_general | solution.py:70
  73.6 11.7 %collective-permute-done.6 = bf16[512,512]{1,0:T(8,128)(2,1)} collective-permute-done((bf16[512,512]{1,0:T(8,128)(2,1)}, bf16[512,512]{1,0:T(8,128)(2,1)}, u32[]{:S(2)}, u32[]{:S(2)}) %collective-permute-start.6) | collective-permute-done | bytes 524320 | tf_op jit(solution)/shard_map/ppermute | solution.py:16
  86.6 5.1 %fusion.17 = f32[2,2,512,256]{2,3,1,0:T(8,128)} fusion(bf16[512,2,256,1]{0,2,3,1:T(8,128)(2,1)S(1)} %bitcast.115, f32[2,2,512,512]{2,3,1,0:T(8,128)} %copy-done.3, f32[2,2,512]{2,1,0:T(2,128)S(1)} %maximum_maximum_fusion, pred[512,512]{0,1:T(8,128)(4,1)S(1)} %get-tuple-element.17), kind=kOutput, calls=%fused_computation.26 | convolution fusion | flops 542113792 | bytes 7086080 | tf_op jit(solution)/shard_map/hmqk,khe->qhme/dot_general | solution.py:70
  92.9 6.0 %add_bitcast_fusion = f32[512,2,2,256]{0,3,2,1:T(8,128)S(1)} fusion(f32[2,2,512,256]{2,3,1,0:T(8,128)} %fusion.17, f32[2,2,512,256]{2,3,1,0:T(8,128)} %fusion.19, f32[2,2,512,256]{2,3,1,0:T(8,128)} %fusion.23, f32[2,2,512,256]{2,3,1,0:T(8,128)S(1)} %fusion.21, bf16[512,2,256,1]{0,2,3,1:T(8,128)(2,1)S(1)} %bitcast.111, f32[2,2,512,512]{2,3,1,0:T(8,128)} %copy-done.2, ...), kind=kOutput, calls=%fused_computation.30 | convolution fusion | flops 544210944 | bytes 15474688 | tf_op jit(solution)/shard_map/hmqk,khe->qhme/dot_general | solution.py:70
  99.9 8.2 %fusion.90 = f32[512,8192]{1,0:T(8,128)} fusion(bf16[512,512]{0,1:T(8,128)(2,1)S(1)} %fusion.59, bf16[512,8192]{1,0:T(8,128)(2,1)S(1)} %bitcast.110), kind=kOutput, calls=%fused_computation.119 | convolution fusion | flops 4294967296 | bytes 25690112 | tf_op jit(solution)/shard_map/dot_general | solution.py:87
  108.1 185.5 %reduce-scatter.2.cloned.1.call-done = f32[32,8192]{1,0:T(8,128)} async-done(((f32[512,8192]{1,0:T(8,128)}), f32[32,8192]{1,0:T(8,128)}) %reduce-scatter.2.cloned.1.call-update) | async-done | bytes 1048592 | tf_op jit(solution)/shard_map/reduce_scatter | solution.py:86
  293.5 2.1 convert_element_type.28
  (62 shorter events, 12.5 us)
Async XLA Ops:
  6.5 24.3 %copy-start = (f32[256]{0:T(256)S(1)}, f32[256]{0:T(256)}, u32[]{:S(2)}) copy-start(f32[256]{0:T(256)} %param.14) | copy-start | bytes 3076
  6.5 21.8 %copy-start.10 = (f32[2,256]{1,0:T(2,128)S(1)}, f32[2,256]{1,0:T(2,128)}, u32[]{:S(2)}) copy-start(f32[2,256]{1,0:T(2,128)} %param.12) | copy-start | bytes 6148
  6.5 21.8 %copy-start.9 = (f32[2,256]{1,0:T(2,128)S(1)}, f32[2,256]{1,0:T(2,128)}, u32[]{:S(2)}) copy-start(f32[2,256]{1,0:T(2,128)} %param.13) | copy-start | bytes 6148
  6.5 287.0 %reduce-scatter.2.cloned.1.call-start = ((), (), s32[]{:S(2)}) async-start(), calls=%async_computation.1 | async-start | bytes 17825792 | tf_op jit(solution)/shard_map/reduce_scatter | solution.py:86
  7.8 23.0 %collective-permute-start.3 = (bf16[512,512]{0,1:T(8,128)(2,1)S(1)}, bf16[512,512]{0,1:T(8,128)(2,1)}, u32[]{:S(2)}, u32[]{:S(2)}) collective-permute-start(bf16[512,512]{0,1:T(8,128)(2,1)S(1)} %copy.53), channel_id=1, source_target_pairs={{0,64},{16,80},{32,96},{48,112},{64,128},{80,144},{96,160},{112,17... | collective-permute-start | bytes 1572872 | tf_op jit(solution)/shard_map/ppermute | solution.py:16
  11.2 25.3 %collective-permute-start.2 = (bf16[512,512]{0,1:T(8,128)(2,1)S(1)}, bf16[512,512]{0,1:T(8,128)(2,1)}, u32[]{:S(2)}, u32[]{:S(2)}) collective-permute-start(bf16[512,512]{0,1:T(8,128)(2,1)S(1)} %copy.53), channel_id=1, source_target_pairs={{0,48},{16,64},{32,80},{48,96},{64,112},{80,128},{96,144},{112,160... | collective-permute-start | bytes 1572872 | tf_op jit(solution)/shard_map/ppermute | solution.py:16
  14.2 31.8 %collective-permute-start.1 = (bf16[512,512]{0,1:T(8,128)(2,1)S(1)}, bf16[512,512]{0,1:T(8,128)(2,1)}, u32[]{:S(2)}, u32[]{:S(2)}) collective-permute-start(bf16[512,512]{0,1:T(8,128)(2,1)S(1)} %copy.53), channel_id=1, source_target_pairs={{0,32},{16,48},{32,64},{48,80},{64,96},{80,112},{96,128},{112,144}... | collective-permute-start | bytes 1572872 | tf_op jit(solution)/shard_map/ppermute | solution.py:16
  18.4 32.8 %collective-permute-start = (bf16[512,512]{0,1:T(8,128)(2,1)S(1)}, bf16[512,512]{0,1:T(8,128)(2,1)}, u32[]{:S(2)}, u32[]{:S(2)}) collective-permute-start(bf16[512,512]{0,1:T(8,128)(2,1)S(1)} %copy.53), channel_id=1, source_target_pairs={{0,16},{16,32},{32,48},{48,64},{64,80},{80,96},{96,112},{112,128},... | collective-permute-start | bytes 1572872 | tf_op jit(solution)/shard_map/ppermute | solution.py:16
  20.3 38.8 %collective-permute-start.4 = (bf16[512,512]{1,0:T(8,128)(2,1)}, bf16[512,512]{1,0:T(8,128)(2,1)S(1)}, u32[]{:S(2)}, u32[]{:S(2)}) collective-permute-start(bf16[512,512]{1,0:T(8,128)(2,1)} %param.10), channel_id=1, source_target_pairs={{0,16},{16,32},{32,48},{48,64},{64,80},{80,96},{96,112},{112,128},... | collective-permute-start | bytes 1572872 | tf_op jit(solution)/shard_map/ppermute | solution.py:16
  30.8 22.9 %copy-start.4 = (f32[2,2,512,512]{2,3,1,0:T(8,128)}, f32[2,2,512,512]{2,3,1,0:T(8,128)S(1)}, u32[]{:S(2)}) copy-start(f32[2,2,512,512]{2,3,1,0:T(8,128)S(1)} %get-tuple-element.28) | copy-start | bytes 12582916
  30.8 36.4 %collective-permute-start.5 = (bf16[512,512]{1,0:T(8,128)(2,1)}, bf16[512,512]{1,0:T(8,128)(2,1)}, u32[]{:S(2)}, u32[]{:S(2)}) collective-permute-start(bf16[512,512]{1,0:T(8,128)(2,1)} %param.10), channel_id=1, source_target_pairs={{0,32},{16,48},{32,64},{48,80},{64,96},{80,112},{96,128},{112,144}... | collective-permute-start | bytes 1572872 | tf_op jit(solution)/shard_map/ppermute | solution.py:16
  36.6 17.1 %copy-start.2 = (f32[2,2,512,512]{2,3,1,0:T(8,128)}, f32[2,2,512,512]{2,3,1,0:T(8,128)S(1)}, u32[]{:S(2)}) copy-start(f32[2,2,512,512]{2,3,1,0:T(8,128)S(1)} %get-tuple-element.22) | copy-start | bytes 12582916
  36.6 48.7 %collective-permute-start.6 = (bf16[512,512]{1,0:T(8,128)(2,1)}, bf16[512,512]{1,0:T(8,128)(2,1)}, u32[]{:S(2)}, u32[]{:S(2)}) collective-permute-start(bf16[512,512]{1,0:T(8,128)(2,1)} %param.10), channel_id=1, source_target_pairs={{0,48},{16,64},{32,80},{48,96},{64,112},{80,128},{96,144},{112,160... | collective-permute-start | bytes 1572872 | tf_op jit(solution)/shard_map/ppermute | solution.py:16
  43.2 10.5 %copy-start.3 = (f32[2,2,512,512]{2,3,1,0:T(8,128)}, f32[2,2,512,512]{2,3,1,0:T(8,128)S(1)}, u32[]{:S(2)}) copy-start(f32[2,2,512,512]{2,3,1,0:T(8,128)S(1)} %get-tuple-element.24) | copy-start | bytes 12582916
  46.0 45.6 %collective-permute-start.7 = (bf16[512,512]{1,0:T(8,128)(2,1)}, bf16[512,512]{1,0:T(8,128)(2,1)}, u32[]{:S(2)}, u32[]{:S(2)}) collective-permute-start(bf16[512,512]{1,0:T(8,128)(2,1)} %param.10), channel_id=1, source_target_pairs={{0,64},{16,80},{32,96},{48,112},{64,128},{80,144},{96,160},{112,17... | collective-permute-start | bytes 1572872 | tf_op jit(solution)/shard_map/ppermute | solution.py:16
  51.2 8.0 %copy-start.6 = (f32[2,2,512,512]{2,3,1,0:T(8,128)}, f32[2,2,512,512]{2,3,1,0:T(8,128)S(1)}, u32[]{:S(2)}) copy-start(f32[2,2,512,512]{2,3,1,0:T(8,128)S(1)} %get-tuple-element.26) | copy-start | bytes 12582916
  53.6 5.5 %copy-start.7 = (f32[2,2,512,512]{2,3,1,0:T(8,128)}, f32[2,2,512,512]{2,3,1,0:T(8,128)S(1)}, u32[]{:S(2)}) copy-start(f32[2,2,512,512]{2,3,1,0:T(8,128)S(1)} %get-tuple-element.30) | copy-start | bytes 12582916
  60.2 4.0 %copy-start.5 = (f32[2,2,512,512]{2,3,1,0:T(8,128)S(1)}, f32[2,2,512,512]{2,3,1,0:T(8,128)}, u32[]{:S(2)}) copy-start(f32[2,2,512,512]{2,3,1,0:T(8,128)} %copy-done.4) | copy-start | bytes 12582916
  60.2 4.0 %copy-start.8 = (bf16[512,512]{0,1:T(8,128)(2,1)S(1)}, bf16[512,512]{0,1:T(8,128)(2,1)}, u32[]{:S(2)}) copy-start(bf16[512,512]{0,1:T(8,128)(2,1)} %copy.90) | copy-start | bytes 1572868
  92.9 6.9 %slice-start = ((s8[8388608]{0:T(1024)(128)(4,1)}), s8[4194304]{0:T(1024)(128)(4,1)S(1)}, s32[]{:S(2)}) async-start(s8[8388608]{0:T(1024)(128)(4,1)} %bitcast.109), calls=%async_computation.2 | async-start | bytes 8388608
  92.9 6.9 %slice-start.1 = ((s8[8388608]{0:T(1024)(128)(4,1)}), s8[4194304]{0:T(1024)(128)(4,1)S(1)}, s32[]{:S(2)}) async-start(s8[8388608]{0:T(1024)(128)(4,1)} %bitcast.109), calls=%async_computation.3 | async-start | bytes 8388608
  108.0 187.5 %copy-start.1 = (f32[256]{0:T(256)S(1)}, f32[256]{0:T(256)}, u32[]{:S(2)}) copy-start(f32[256]{0:T(256)} %param.14) | copy-start | bytes 3076
Sparse Core Ops, SparseCore 0:
  108.2 185.2 reduce-scatter.1
where the time goes:
time: 308 us; the launch traced here: 302 us
  waiting for transfers between devices  200 us (65%)
  matrix products  40.9 us (13%)
  starting transfers between devices  26.6 us (9%)
  between operations  13.8 us (4%)
  local copies, waits for them, and re-layouts  10.8 us (4%)
  other arithmetic  10.2 us (3%)
    reduce_scatter x1, waiting for transfers between devices, shards(): lax.psum_scatter(jnp.dot(attended, out_weight, preferred_element_type=jnp...  185 us
    ppermute x8, starting transfers between devices, shifted(): lax.ppermute(value, axis, [(source, source + steps) for source in range(f...  26.6 us
    dot_general x5, matrix products, make_product(): jnp.einsum('hmqk,khe->qhme', rounded, value_three, preferred_element_type...  23.2 us
    ppermute x8, waiting for transfers between devices, shifted(): lax.ppermute(value, axis, [(source, source + steps) for source in range(f...  14.6 us
    dot_general x5, matrix products, make_scores(): jnp.einsum('qhmd,khmd->hmqk', query_four, key_four, preferred_element_typ...  9.55 us
    dot_general x1, matrix products, shards(): jnp.dot(attended, out_weight, preferred_element_type=jnp.float32)  8.17 us
  transfers between devices with their start and end apart: 9, of which 3 were waited for; matrix products, arithmetic and copies ran while one was open for 14% of the time, Pallas kernels for 0%

commit v1 on v0

v1 whole, which is shorter than its diff:
```python
import functools
import math

import jax
import jax.numpy as jnp
from jax import lax
from jax.experimental import pallas as pl
from jax.experimental.pallas import tpu as pltpu
from jax.sharding import PartitionSpec as P

EPS = 1e-05
LAMBDA_INIT = 0.8 - 0.6 * math.exp(-3.3)
NEG = -1e30
HD = 128
TOK = 512
TILE = 256
GROUP = 4
MIB = 1024 * 1024


def segments(tile):
    first = tile * TILE
    parts = [(0, 0, first + TILE)]
    parts += [(offset, 0, TOK) for offset in (1, 2, 3)]
    parts.append((4, first, TOK))
    return parts


def attention_kernel(start_ref, lambda_ref, gain_ref, q_ref, *refs):
    blocks, out_ref, score_ref = refs[:5], refs[5], refs[6]
    factor = HD**-0.5 * math.log2(math.e)
    for tile in range(TOK // TILE):
        rows = pl.ds(tile * TILE, TILE)
        starts = start_ref[rows, :]
        ratio = []
        for which in range(2):
            columns = slice(which * HD, (which + 1) * HD)
            query = q_ref[rows, columns]
            best = jnp.full((TILE, HD), NEG, jnp.float32)
            at = 0
            places = []
            for offset, low, high in segments(tile):
                size = high - low
                score = (
                    lax.dot_general(
                        query,
                        blocks[offset][low:high, columns],
                        (((1,), (1,)), ((), ())),
                        preferred_element_type=jnp.float32,
                    )
                    * factor
                )
                key = lax.broadcasted_iota(jnp.int32, (TILE, size), 1) + (low - offset * TOK)
                live = key >= starts
                if offset == 0:
                    token = lax.broadcasted_iota(jnp.int32, (TILE, size), 0) + tile * TILE
                    live = live & (key <= token)
                score = jnp.where(live, score, NEG)
                score_ref[:, at : at + size] = score
                for piece in range(0, size, HD):
                    best = jnp.maximum(best, score[:, piece : piece + HD])
                places.append((offset, low, high, at))
                at += size
            row_max = jnp.max(best, axis=1, keepdims=True)
            total = jnp.zeros((TILE, HD), jnp.float32)
            summed = jnp.zeros((TILE, 2 * HD), jnp.float32)
            for offset, low, high, at in places:
                size = high - low
                weight = jnp.exp2(score_ref[:, at : at + size] - row_max)
                for piece in range(0, size, HD):
                    total = total + weight[:, piece : piece + HD]
                summed = summed + jnp.dot(
                    weight.astype(jnp.bfloat16),
                    blocks[offset][low:high, 2 * HD :],
                    preferred_element_type=jnp.float32,
                )
            ratio.append(summed / jnp.sum(total, axis=1, keepdims=True))
        combined = ratio[0] - lambda_ref[0] * ratio[1]
        power = jnp.mean(combined * combined, axis=1, keepdims=True)
        out_ref[rows, :] = (
            combined * lax.rsqrt(power + EPS) * gain_ref[...] * (1.0 - LAMBDA_INIT)
        ).astype(jnp.bfloat16)


def attention(starts, scale, gain, query, blocks):
    vmem = pl.BlockSpec(memory_space=pltpu.VMEM)
    return pl.pallas_call(
        attention_kernel,
        out_shape=jax.ShapeDtypeStruct((TOK, 2 * HD), jnp.bfloat16),
        in_specs=[vmem, pl.BlockSpec(memory_space=pltpu.SMEM)] + [vmem] * 7,
        out_specs=vmem,
        scratch_shapes=[pltpu.VMEM((TILE, 5 * TOK), jnp.float32)],
        compiler_params=pltpu.CompilerParams(vmem_limit_bytes=24 * MIB),
        cost_estimate=pl.CostEstimate(
            flops=2 * 2 * TOK * 5 * TOK * 3 * HD, bytes_accessed=3 * MIB, transcendentals=2 * TOK * 5 * TOK
        ),
    )(starts, scale, gain, query, *blocks)


def project_kernel(*refs):
    attended, weights, out_ref = refs[:8], refs[8:16], refs[16]
    half = weights[0].shape[1]
    step = 256
    for side in range(2):
        for column in range(0, half, step):
            total = None
            for member in range(4):
                for head in range(2):
                    term = jnp.dot(
                        attended[member * 2 + head][...],
                        weights[side * 4 + member][head * 256 : (head + 1) * 256, column : column + step],
                        preferred_element_type=jnp.float32,
                    )
                    total = term if total is None else total + term
            out_ref[:, side * half + column : side * half + column + step] = total.astype(jnp.bfloat16)


def project(attended, weights):
    vmem = pl.BlockSpec(memory_space=pltpu.VMEM)
    half = weights[0].shape[1]
    return pl.pallas_call(
        project_kernel,
        out_shape=jax.ShapeDtypeStruct((TOK, 2 * half), jnp.bfloat16),
        in_specs=[vmem] * 16,
        out_specs=vmem,
        compiler_params=pltpu.CompilerParams(vmem_limit_bytes=32 * MIB),
        cost_estimate=pl.CostEstimate(
            flops=2 * TOK * 2048 * 2 * half, bytes_accessed=12 * MIB, transcendentals=0
        ),
    )(*attended, *weights)


def total_kernel(core_ref, parts_ref, out_ref):
    half = parts_ref.shape[2] // 2
    for member in range(4):
        high, low = divmod(member, 2)
        for side in range(2):
            total = None
            for pair in range(4):
                source = high * 8 + pair * 2 + low
                term = parts_ref[source, :, side * half : (side + 1) * half].astype(jnp.float32)
                total = term if total is None else total + term
            place = member * 2 * half + (core_ref[0] if side == 0 else 1 - core_ref[0]) * half
            out_ref[:, pl.ds(pl.multiple_of(place, half), half)] = total.astype(jnp.bfloat16)


def total_up(core, parts):
    vmem = pl.BlockSpec(memory_space=pltpu.VMEM)
    return pl.pallas_call(
        total_kernel,
        out_shape=jax.ShapeDtypeStruct((parts.shape[1], 4 * parts.shape[2]), jnp.bfloat16),
        in_specs=[pl.BlockSpec(memory_space=pltpu.SMEM), vmem],
        out_specs=vmem,
        compiler_params=pltpu.CompilerParams(vmem_limit_bytes=16 * MIB),
    )(core, parts)


def later(value, steps):
    count = lax.axis_size("ctx")
    return lax.ppermute(value, "ctx", [(i, i + steps) for i in range(count - steps)])


def across(value):
    return lax.ppermute(value, "ctx", [(i, i ^ 1) for i in range(lax.axis_size("ctx"))])


def partner(value, member):
    high, low = divmod(member, 2)
    pairs = [(t, (((t // 8) ^ high) * 8) + ((t % 8) ^ low)) for t in range(lax.axis_size("tp"))]
    return lax.ppermute(value, "tp", pairs)


def shards(queries, keys, values, positions, lambda_query, lambda_key, norm_gain, out_weight):
    ctx = lax.axis_index("ctx")
    tp = lax.axis_index("tp")
    core = lax.rem(ctx, 2)
    own = (tp // 8) * 2 + lax.rem(tp, 2)
    starts = (jnp.arange(TOK, dtype=jnp.int32) - positions)[:, None]
    lambda_head = (
        jnp.exp(jnp.sum(lambda_query[:, :HD] * lambda_key[:, :HD], axis=1))
        - jnp.exp(jnp.sum(lambda_query[:, HD:] * lambda_key[:, HD:], axis=1))
        + LAMBDA_INIT
    )
    gain = norm_gain[None, :]
    width = 2 * HD

    pairs = []
    for head in range(2):
        part = slice(head * width, (head + 1) * width)
        here = jnp.concatenate([keys[:, part], values[:, part]], axis=1)
        pairs.append((here, later(here, 2), later(here, 4)))

    side = out_weight.shape[1] // GROUP // 2

    def weight_part(member, half):
        place = (own ^ member) * (2 * side) + half * side
        return lax.dynamic_slice(out_weight, (0, place), (out_weight.shape[0], side))

    mine = [weight_part(0, core)] + [partner(weight_part(d, core), d) for d in (1, 2, 3)]
    other = [weight_part(0, 1 - core)] + [across(piece) for piece in mine[1:]]

    attended = []
    for head in range(2):
        here, two, four = pairs[head]
        even = core == 0
        one, three = across((jnp.where(even, here, two), jnp.where(even, two, four)))
        result = attention(
            starts,
            lambda_head[head : head + 1],
            gain,
            queries[:, head * width : (head + 1) * width],
            [here, one, two, three, four],
        )
        attended.append([result] + [partner(result, d) for d in (1, 2, 3)])
    flat = [attended[head][member] for member in range(4) for head in range(2)]
    partial = project(flat, mine + other)
    count = lax.axis_size("tp")
    parts = lax.all_to_all(partial.reshape(count, TOK // count, 2 * side), "tp", 0, 0)
    return total_up(core[None], parts)


def solution(mesh):
    return jax.shard_map(
        shards,
        mesh=mesh,
        in_specs=(
            P("ctx", "tp"),
            P("ctx", "tp"),
            P("ctx", "tp"),
            P("ctx"),
            P("tp", None),
            P("tp", None),
            P(),
            P("tp", None),
        ),
        out_specs=P(("ctx", "tp"), None),
        check_vma=False,
    )
```

time: 308 us -> 189 us (0.61); the launches traced: 302 us -> 189 us
  waiting for transfers between devices: 200 us -> 77.5 us
  blocking collectives: 0 us -> 57.5 us
  matrix products: 40.9 us -> 0 us
  Pallas kernels: 0 us -> 20.8 us
  between operations: 13.8 us -> 0.23 us
  other arithmetic: 10.2 us -> 3.93 us
  starting transfers between devices: 26.6 us -> 21.3 us
  local copies, waits for them, and re-layouts: 10.8 us -> 7.69 us
    reduce_scatter x1 -> x0, waiting for transfers between devices: 185 us -> none  [shards(): lax.psum_scatter(jnp.dot(attended, out_weight, preferred_element_type=jnp...]
    ppermute x8 -> x20, waiting for transfers between devices: 14.6 us -> 77.5 us  [the longest x9 42.3 us: partner(): return lax.ppermute(value, 'tp', pairs)]
    all_to_all x0 -> x1, blocking collectives: none -> 57.5 us  [shards(): lax.all_to_all(partial.reshape(count, TOK // count, 2 * side), 'tp', 0, 0)]
    dot_general x11 -> x0, matrix products: 40.9 us -> none  [the longest x5 23.2 us: make_product(): jnp.einsum('hmqk,khe->qhme', rounded, value_three, preferred_element_type...]
    pallas_call x0 -> x4, Pallas kernels: none -> 20.8 us  [the longest x2 13.4 us: attention(): pl.pallas_call(attention_kernel, out_shape=jax.ShapeDtypeStruct((TOK, 2 *...]
    reduce_sum x3 -> x1, other arithmetic: 5.89 us -> 0.14 us  [shards(): jnp.sum(lambda_query[:, :HD] * lambda_key[:, :HD], axis=1)]
    ppermute x8 -> x20, starting transfers between devices: 26.6 us -> 21.3 us  [the longest x4 13.3 us: later(): lax.ppermute(value, 'ctx', [(i, i + steps) for i in range(count - steps)])]
    ppermute x4 -> x0, local copies, waits for them, and re-layouts: 4.79 us -> none  [shifted(): lax.ppermute(value, axis, [(source, source + steps) for source in range(f...]
  transfers between devices with their start and end apart: 9 -> 20, of which waited for: 3 -> 10; matrix products, arithmetic and copies ran while one was open for 14% -> 5% of each run, Pallas kernels for 0% -> 7%
where the time goes in v1:
time: 189 us
  waiting for transfers between devices  77.5 us (41%)
  blocking collectives  57.5 us (30%)
  starting transfers between devices  21.3 us (11%)
  Pallas kernels  20.8 us (11%)
  local copies, waits for them, and re-layouts  7.69 us (4%)
  other arithmetic  3.93 us (2%)
    all_to_all x1, blocking collectives, shards(): lax.all_to_all(partial.reshape(count, TOK // count, 2 * side), 'tp', 0, 0)  57.5 us
    ppermute x9, waiting for transfers between devices, partner(): return lax.ppermute(value, 'tp', pairs)  42.3 us
    ppermute x4, waiting for transfers between devices, later(): lax.ppermute(value, 'ctx', [(i, i + steps) for i in range(count - steps)])  35.2 us
    pallas_call x2, Pallas kernels, attention(): pl.pallas_call(attention_kernel, out_shape=jax.ShapeDtypeStruct((TOK, 2 *...  13.4 us
    ppermute x4, starting transfers between devices, later(): lax.ppermute(value, 'ctx', [(i, i + steps) for i in range(count - steps)])  13.3 us
    ppermute x9, starting transfers between devices, partner(): return lax.ppermute(value, 'tp', pairs)  6.53 us
    pallas_call x1, Pallas kernels, project(): pl.pallas_call(project_kernel, out_shape=jax.ShapeDtypeStruct((TOK, 2 * h...  6.35 us
    dynamic_slice x1, local copies, waits for them, and re-layouts, weight_part(): lax.dynamic_slice(out_weight, (0, place), (out_weight.shape[0], side))  4.55 us
  transfers between devices with their start and end apart: 20, of which 10 were waited for; matrix products, arithmetic and copies ran while one was open for 5% of the time, Pallas kernels for 7%

profile of v1, /device:TPU:58, one launch (start us, length us, event | category | flops | bytes accessed | tf_op | source)
XLA Modules:
  0.0 188.9 jit_solution(12707560336674806383)
XLA Ops:
  0.0 1.3 fusion
  1.4 3.4 %collective-permute-start.2 = (bf16[512,512]{1,0:T(8,128)(2,1)S(1)}, bf16[512,512]{1,0:T(8,128)(2,1)}, u32[]{:S(2)}, u32[]{:S(2)}) collective-permute-start(bf16[512,512]{1,0:T(8,128)(2,1)S(1)} %pad_maximum_fusion.refs_0_), channel_id=1, source_target_pairs={{0,64},{16,80},{32,96},{48,112},{64,128},{80,144},{96,160},{112,17... | collective-permute-start | bytes 1572872 | tf_op jit(solution)/shard_map/ppermute | solution.py:160
  4.8 3.8 %collective-permute-start = (bf16[512,512]{1,0:T(8,128)(2,1)S(1)}, bf16[512,512]{1,0:T(8,128)(2,1)}, u32[]{:S(2)}, u32[]{:S(2)}) collective-permute-start(bf16[512,512]{1,0:T(8,128)(2,1)S(1)} %pad_maximum_fusion.refs_0_), channel_id=1, source_target_pairs={{0,32},{16,48},{32,64},{48,80},{64,96},{80,112},{96,128},{112,144}... | collective-permute-start | bytes 1572872 | tf_op jit(solution)/shard_map/ppermute | solution.py:160
  8.6 1.9 %collective-permute-start.6 = (bf16[512,512]{1,0:T(8,128)(2,1)S(1)}, bf16[512,512]{1,0:T(8,128)(2,1)}, u32[]{:S(2)}, u32[]{:S(2)}) collective-permute-start(bf16[512,512]{1,0:T(8,128)(2,1)S(1)} %pad_maximum_fusion.1.refs_0_), channel_id=1, source_target_pairs={{0,64},{16,80},{32,96},{48,112},{64,128},{80,144},{96,160},{112,17... | collective-permute-start | bytes 1572872 | tf_op jit(solution)/shard_map/ppermute | solution.py:160
  10.6 4.2 %collective-permute-start.4 = (bf16[512,512]{1,0:T(8,128)(2,1)S(1)}, bf16[512,512]{1,0:T(8,128)(2,1)}, u32[]{:S(2)}, u32[]{:S(2)}) collective-permute-start(bf16[512,512]{1,0:T(8,128)(2,1)S(1)} %pad_maximum_fusion.1.refs_0_), channel_id=1, source_target_pairs={{0,32},{16,48},{32,64},{48,80},{64,96},{80,112},{96,128},{112,144}... | collective-permute-start | bytes 1572872 | tf_op jit(solution)/shard_map/ppermute | solution.py:160
  14.8 4.5 %constant_dynamic-slice_fusion = (bf16[512,1024]{1,0:T(8,128)(2,1)S(1)}, bf16[512,1024]{1,0:T(8,128)(2,1)}, bf16[512,1024]{1,0:T(8,128)(2,1)}, bf16[512,1024]{1,0:T(8,128)(2,1)S(1)}, bf16[512,1024]{1,0:T(8,128)(2,1)}) fusion(bf16[512,8192]{1,0:T(8,128)(2,1)} %param.15, s32[]{:T(128)S(6)} %select_n.50, s32[]{:T(128)S(6)} %select_n.48, s32[]{:T(128)S(6)} %select_n.47, ...), kind=kLoop, calls=%fused_computation.7 | loop fusion | bytes 10485780 | tf_op jit(solution)/shard_map/dynamic_slice | solution.py:197
  20.3 8.0 %collective-permute-done.refs_2_ = bf16[512,512]{1,0:T(8,128)(2,1)} collective-permute-done((bf16[512,512]{1,0:T(8,128)(2,1)S(1)}, bf16[512,512]{1,0:T(8,128)(2,1)}, u32[]{:S(2)}, u32[]{:S(2)}) %collective-permute-start) | collective-permute-done | bytes 524320 | tf_op jit(solution)/shard_map/ppermute | solution.py:160
  28.7 2.3 %broadcast_select_fusion.2 = (bf16[512,512]{1,0:T(8,128)(2,1)}, bf16[512,512]{1,0:T(8,128)(2,1)}) fusion(bf16[512,512]{1,0:T(8,128)(2,1)} %collective-permute-done.refs_2_, bf16[512,512]{1,0:T(8,128)(2,1)} %collective-permute-done.2.refs_4_, pred[]{:T(512)S(6)} %eq.4, bf16[512,256]{1,0:T(8,128)(2,1)} %copy-done.3, bf16[512,256]{1,0:T(8,128)(2,1)S(1)} %get-tuple-element.15), kind=kLoop, calls=%fused_computation.4 | loop fusion | flops 1572864 | bytes 2621441 | tf_op jit(solution)/shard_map/jit(_where)/select_n | solution.py:206
  31.0 9.7 %collective-permute-done.6.refs_4_ = bf16[512,512]{1,0:T(8,128)(2,1)} collective-permute-done((bf16[512,512]{1,0:T(8,128)(2,1)S(1)}, bf16[512,512]{1,0:T(8,128)(2,1)}, u32[]{:S(2)}, u32[]{:S(2)}) %collective-permute-start.6) | collective-permute-done | bytes 524320 | tf_op jit(solution)/shard_map/ppermute | solution.py:160
  40.7 17.4 %collective-permute-done.4.refs_2_ = bf16[512,512]{1,0:T(8,128)(2,1)} collective-permute-done((bf16[512,512]{1,0:T(8,128)(2,1)S(1)}, bf16[512,512]{1,0:T(8,128)(2,1)}, u32[]{:S(2)}, u32[]{:S(2)}) %collective-permute-start.4) | collective-permute-done | bytes 524320 | tf_op jit(solution)/shard_map/ppermute | solution.py:160
  59.5 1.4 broadcast_select_fusion
  61.8 22.8 %collective-permute-done.15.refs_10_ = bf16[512,1024]{1,0:T(8,128)(2,1)} collective-permute-done((bf16[512,1024]{1,0:T(8,128)(2,1)}, bf16[512,1024]{1,0:T(8,128)(2,1)}, u32[]{:S(2)}, u32[]{:S(2)}) %collective-permute-start.15) | collective-permute-done | bytes 1048608 | tf_op jit(solution)/shard_map/ppermute | solution.py:170
  85.8 6.9 %shard_map.82.refs_0_ = bf16[512,256]{1,0:T(8,128)(2,1)S(1)} custom-call(s32[512,1]{1,0:T(8,128)S(1)} %copy.9.start_ref, f32[1]{0:T(128)} %get-tuple-element.23.lambda_ref, f32[1,256]{1,0:T(1,128)S(1)} %bitcast.5, bf16[512,256]{1,0:T(8,128)(2,1)S(1)} %get-tuple-element.19.q_ref, bf16[512,512]{1,0:T(8,128)(2,1)S(1)} %pad_maximum_fusion.refs_0_, ...), custom_call_target="tpu_custom_call" | custom-call | flops 2013265920 | bytes 3145728 | tf_op jit(solution)/shard_map/pallas_call | solution.py:87
  92.7 1.1 collective-permute-start.12
  94.6 6.5 %shard_map.83.refs_1_ = bf16[512,256]{1,0:T(8,128)(2,1)S(1)} custom-call(s32[512,1]{1,0:T(8,128)S(1)} %copy.9.start_ref, f32[1]{0:T(128)} %get-tuple-element.22.lambda_ref, f32[1,256]{1,0:T(1,128)S(1)} %bitcast.6, bf16[512,256]{1,0:T(8,128)(2,1)S(1)} %get-tuple-element.18.q_ref, bf16[512,512]{1,0:T(8,128)(2,1)S(1)} %pad_maximum_fusion.1.refs_0_, ...), custom_call_target="tpu_custom_call" | custom-call | flops 2013265920 | bytes 3145728 | tf_op jit(solution)/shard_map/pallas_call | solution.py:87
  101.1 1.6 collective-permute-done.12.refs_6_
  103.1 4.7 %collective-permute-done.10.refs_4_ = bf16[512,256]{1,0:T(8,128)(2,1)S(1)} collective-permute-done((bf16[512,256]{1,0:T(8,128)(2,1)S(1)}, bf16[512,256]{1,0:T(8,128)(2,1)S(1)}, u32[]{:S(2)}, u32[]{:S(2)}) %collective-permute-start.10) | collective-permute-done | bytes 262176 | tf_op jit(solution)/shard_map/ppermute | solution.py:170
  107.8 1.2 collective-permute-start.13
  109.0 1.7 collective-permute-done.8.refs_2_
  111.8 5.1 %collective-permute-done.13.refs_7_ = bf16[512,256]{1,0:T(8,128)(2,1)S(1)} collective-permute-done((bf16[512,256]{1,0:T(8,128)(2,1)S(1)}, bf16[512,256]{1,0:T(8,128)(2,1)S(1)}, u32[]{:S(2)}, u32[]{:S(2)}) %collective-permute-start.13) | collective-permute-done | bytes 262176 | tf_op jit(solution)/shard_map/ppermute | solution.py:170
  117.6 4.8 %collective-permute-done.11.refs_5_ = bf16[512,256]{1,0:T(8,128)(2,1)S(1)} collective-permute-done((bf16[512,256]{1,0:T(8,128)(2,1)S(1)}, bf16[512,256]{1,0:T(8,128)(2,1)S(1)}, u32[]{:S(2)}, u32[]{:S(2)}) %collective-permute-start.11) | collective-permute-done | bytes 262176 | tf_op jit(solution)/shard_map/ppermute | solution.py:170
  122.4 1.6 collective-permute-done.9.refs_3_
  124.0 6.3 %shard_map.84 = bf16[512,2048]{1,0:T(8,128)(2,1)S(1)} custom-call(bf16[512,256]{1,0:T(8,128)(2,1)S(1)} %shard_map.82.refs_0_, bf16[512,256]{1,0:T(8,128)(2,1)S(1)} %shard_map.83.refs_1_, bf16[512,256]{1,0:T(8,128)(2,1)S(1)} %collective-permute-done.8.refs_2_, bf16[512,256]{1,0:T(8,128)(2,1)S(1)} %collective-permute-done.9.refs_3_, ...), custom_call_target="tpu_custom_call" | custom-call | flops 4294967296 | bytes 12582912 | tf_op jit(solution)/shard_map/pallas_call | solution.py:121
  130.4 57.5 %all_to_all.5.parts_ref = bf16[16,32,2048]{2,1,0:T(8,128)(2,1)S(1)} all-to-all(bf16[16,32,2048]{2,1,0:T(8,128)(2,1)S(1)} %bitcast.4), channel_id=1, replica_groups=mesh['ctx'=16,'tp'=16] {'tp'}, dimensions={0} | all-to-all | bytes 4194304 | tf_op jit(solution)/shard_map/all_to_all | solution.py:218
  (47 shorter events, 8.9 us)
Async XLA Ops:
  0.0 20.1 %copy-start.4 = (s32[512]{0:T(512)S(1)}, s32[512]{0:T(512)}, u32[]{:S(2)}) copy-start(s32[512]{0:T(512)} %param.11) | copy-start | bytes 6148
  0.0 58.1 %copy-start.5 = (f32[2,256]{1,0:T(2,128)S(1)}, f32[2,256]{1,0:T(2,128)}, u32[]{:S(2)}) copy-start(f32[2,256]{1,0:T(2,128)} %param.13) | copy-start | bytes 6148
  0.0 58.1 %copy-start.6 = (f32[2,256]{1,0:T(2,128)S(1)}, f32[2,256]{1,0:T(2,128)}, u32[]{:S(2)}) copy-start(f32[2,256]{1,0:T(2,128)} %param.12) | copy-start | bytes 6148
  1.4 18.8 %collective-permute-start.2 = (bf16[512,512]{1,0:T(8,128)(2,1)S(1)}, bf16[512,512]{1,0:T(8,128)(2,1)}, u32[]{:S(2)}, u32[]{:S(2)}) collective-permute-start(bf16[512,512]{1,0:T(8,128)(2,1)S(1)} %pad_maximum_fusion.refs_0_), channel_id=1, source_target_pairs={{0,64},{16,80},{32,96},{48,112},{64,128},{80,144},{96,160},{112,17... | collective-permute-start | bytes 1572872 | tf_op jit(solution)/shard_map/ppermute | solution.py:160
  4.8 23.6 %collective-permute-start = (bf16[512,512]{1,0:T(8,128)(2,1)S(1)}, bf16[512,512]{1,0:T(8,128)(2,1)}, u32[]{:S(2)}, u32[]{:S(2)}) collective-permute-start(bf16[512,512]{1,0:T(8,128)(2,1)S(1)} %pad_maximum_fusion.refs_0_), channel_id=1, source_target_pairs={{0,32},{16,48},{32,64},{48,80},{64,96},{80,112},{96,128},{112,144}... | collective-permute-start | bytes 1572872 | tf_op jit(solution)/shard_map/ppermute | solution.py:160
  8.6 32.1 %collective-permute-start.6 = (bf16[512,512]{1,0:T(8,128)(2,1)S(1)}, bf16[512,512]{1,0:T(8,128)(2,1)}, u32[]{:S(2)}, u32[]{:S(2)}) collective-permute-start(bf16[512,512]{1,0:T(8,128)(2,1)S(1)} %pad_maximum_fusion.1.refs_0_), channel_id=1, source_target_pairs={{0,64},{16,80},{32,96},{48,112},{64,128},{80,144},{96,160},{112,17... | collective-permute-start | bytes 1572872 | tf_op jit(solution)/shard_map/ppermute | solution.py:160
  10.6 47.5 %collective-permute-start.4 = (bf16[512,512]{1,0:T(8,128)(2,1)S(1)}, bf16[512,512]{1,0:T(8,128)(2,1)}, u32[]{:S(2)}, u32[]{:S(2)}) collective-permute-start(bf16[512,512]{1,0:T(8,128)(2,1)S(1)} %pad_maximum_fusion.1.refs_0_), channel_id=1, source_target_pairs={{0,32},{16,48},{32,64},{48,80},{64,96},{80,112},{96,128},{112,144}... | collective-permute-start | bytes 1572872 | tf_op jit(solution)/shard_map/ppermute | solution.py:160
  14.8 71.0 %copy-start = (f32[256]{0:T(256)S(1)}, f32[256]{0:T(256)}, u32[]{:S(2)}) copy-start(f32[256]{0:T(256)} %param.14) | copy-start | bytes 3076
  19.4 65.2 %collective-permute-start.15 = (bf16[512,1024]{1,0:T(8,128)(2,1)}, bf16[512,1024]{1,0:T(8,128)(2,1)}, u32[]{:S(2)}, u32[]{:S(2)}) collective-permute-start(bf16[512,1024]{1,0:T(8,128)(2,1)} %get-tuple-element.8), channel_id=1, source_target_pairs={{0,8},{1,9},{2,10},{3,11},{4,12},{5,13},{6,14},{7,15},{8,0},{9,1},... | collective-permute-start | bytes 3145736 | tf_op jit(solution)/shard_map/ppermute | solution.py:170
  20.2 64.5 %collective-permute-start.14 = (bf16[512,1024]{1,0:T(8,128)(2,1)}, bf16[512,1024]{1,0:T(8,128)(2,1)}, u32[]{:S(2)}, u32[]{:S(2)}) collective-permute-start(bf16[512,1024]{1,0:T(8,128)(2,1)} %get-tuple-element.9), channel_id=1, source_target_pairs={{0,1},{1,0},{2,3},{3,2},{4,5},{5,4},{6,7},{7,6},{8,9},{9,8},{10,11... | collective-permute-start | bytes 3145736 | tf_op jit(solution)/shard_map/ppermute | solution.py:170
  28.4 56.8 %collective-permute-start.16 = (bf16[512,1024]{1,0:T(8,128)(2,1)}, bf16[512,1024]{1,0:T(8,128)(2,1)}, u32[]{:S(2)}, u32[]{:S(2)}) collective-permute-start(bf16[512,1024]{1,0:T(8,128)(2,1)} %get-tuple-element.11), channel_id=1, source_target_pairs={{0,9},{1,8},{2,11},{3,10},{4,13},{5,12},{6,15},{7,14},{8,1},{9,0},... | collective-permute-start | bytes 3145736 | tf_op jit(solution)/shard_map/ppermute | solution.py:170
  40.7 20.2 %collective-permute-start.3 = (bf16[512,512]{1,0:T(8,128)(2,1)}, bf16[512,512]{1,0:T(8,128)(2,1)}, u32[]{:S(2)}, u32[]{:S(2)}) collective-permute-start(bf16[512,512]{1,0:T(8,128)(2,1)} %get-tuple-element.20), channel_id=1, source_target_pairs={{0,16},{16,0},{32,48},{48,32},{64,80},{80,64},{96,112},{112,96},{1... | collective-permute-start | bytes 1572872 | tf_op jit(solution)/shard_map/ppermute | solution.py:164
  58.1 3.6 %collective-permute-start.1 = (bf16[512,512]{1,0:T(8,128)(2,1)}, bf16[512,512]{1,0:T(8,128)(2,1)}, u32[]{:S(2)}, u32[]{:S(2)}) collective-permute-start(bf16[512,512]{1,0:T(8,128)(2,1)} %get-tuple-element.21), channel_id=1, source_target_pairs={{0,16},{16,0},{32,48},{48,32},{64,80},{80,64},{96,112},{112,96},{1... | collective-permute-start | bytes 1572872 | tf_op jit(solution)/shard_map/ppermute | solution.py:164
  60.9 31.8 %collective-permute-start.7 = (bf16[512,512]{1,0:T(8,128)(2,1)S(1)}, bf16[512,512]{1,0:T(8,128)(2,1)S(1)}, u32[]{:S(2)}, u32[]{:S(2)}) collective-permute-start(bf16[512,512]{1,0:T(8,128)(2,1)S(1)} %get-tuple-element.12), channel_id=1, source_target_pairs={{0,16},{16,0},{32,48},{48,32},{64,80},{80,64},{96,112},{112,96},{1... | collective-permute-start | bytes 1572872 | tf_op jit(solution)/shard_map/ppermute | solution.py:164
  61.7 32.1 %collective-permute-start.5 = (bf16[512,512]{1,0:T(8,128)(2,1)S(1)}, bf16[512,512]{1,0:T(8,128)(2,1)S(1)}, u32[]{:S(2)}, u32[]{:S(2)}) collective-permute-start(bf16[512,512]{1,0:T(8,128)(2,1)S(1)} %get-tuple-element.13), channel_id=1, source_target_pairs={{0,16},{16,0},{32,48},{48,32},{64,80},{80,64},{96,112},{112,96},{1... | collective-permute-start | bytes 1572872 | tf_op jit(solution)/shard_map/ppermute | solution.py:164
  84.6 39.4 %collective-permute-start.18 = (bf16[512,1024]{1,0:T(8,128)(2,1)}, bf16[512,1024]{1,0:T(8,128)(2,1)S(1)}, u32[]{:S(2)}, u32[]{:S(2)}) collective-permute-start(bf16[512,1024]{1,0:T(8,128)(2,1)} %collective-permute-done.15.refs_10_), channel_id=1, source_target_pairs={{0,16},{16,0},{32,48},{48,32},{64,80},{80,64},{96,112},{112,96},{1... | collective-permute-start | bytes 3145736 | tf_op jit(solution)/shard_map/ppermute | solution.py:164
  84.7 39.4 %collective-permute-start.17 = (bf16[512,1024]{1,0:T(8,128)(2,1)}, bf16[512,1024]{1,0:T(8,128)(2,1)S(1)}, u32[]{:S(2)}, u32[]{:S(2)}) collective-permute-start(bf16[512,1024]{1,0:T(8,128)(2,1)} %collective-permute-done.14.refs_9_), channel_id=1, source_target_pairs={{0,16},{16,0},{32,48},{48,32},{64,80},{80,64},{96,112},{112,96},{1... | collective-permute-start | bytes 3145736 | tf_op jit(solution)/shard_map/ppermute | solution.py:164
  85.2 38.9 %collective-permute-start.19 = (bf16[512,1024]{1,0:T(8,128)(2,1)}, bf16[512,1024]{1,0:T(8,128)(2,1)S(1)}, u32[]{:S(2)}, u32[]{:S(2)}) collective-permute-start(bf16[512,1024]{1,0:T(8,128)(2,1)} %collective-permute-done.16.refs_11_), channel_id=1, source_target_pairs={{0,16},{16,0},{32,48},{48,32},{64,80},{80,64},{96,112},{112,96},{1... | collective-permute-start | bytes 3145736 | tf_op jit(solution)/shard_map/ppermute | solution.py:164
  92.7 9.9 %collective-permute-start.12 = (bf16[512,256]{1,0:T(8,128)(2,1)S(1)}, bf16[512,256]{1,0:T(8,128)(2,1)S(1)}, u32[]{:S(2)}, u32[]{:S(2)}) collective-permute-start(bf16[512,256]{1,0:T(8,128)(2,1)S(1)} %shard_map.82.refs_0_), channel_id=1, source_target_pairs={{0,9},{1,8},{2,11},{3,10},{4,13},{5,12},{6,15},{7,14},{8,1},{9,0},... | collective-permute-start | bytes 786440 | tf_op jit(solution)/shard_map/ppermute | solution.py:170
  93.8 14.0 %collective-permute-start.10 = (bf16[512,256]{1,0:T(8,128)(2,1)S(1)}, bf16[512,256]{1,0:T(8,128)(2,1)S(1)}, u32[]{:S(2)}, u32[]{:S(2)}) collective-permute-start(bf16[512,256]{1,0:T(8,128)(2,1)S(1)} %shard_map.82.refs_0_), channel_id=1, source_target_pairs={{0,8},{1,9},{2,10},{3,11},{4,12},{5,13},{6,14},{7,15},{8,0},{9,1},... | collective-permute-start | bytes 786440 | tf_op jit(solution)/shard_map/ppermute | solution.py:170
  102.7 8.1 %collective-permute-start.8 = (bf16[512,256]{1,0:T(8,128)(2,1)S(1)}, bf16[512,256]{1,0:T(8,128)(2,1)S(1)}, u32[]{:S(2)}, u32[]{:S(2)}) collective-permute-start(bf16[512,256]{1,0:T(8,128)(2,1)S(1)} %shard_map.82.refs_0_), channel_id=1, source_target_pairs={{0,1},{1,0},{2,3},{3,2},{4,5},{5,4},{6,7},{7,6},{8,9},{9,8},{10,11... | collective-permute-start | bytes 786440 | tf_op jit(solution)/shard_map/ppermute | solution.py:170
  107.8 9.1 %collective-permute-start.13 = (bf16[512,256]{1,0:T(8,128)(2,1)S(1)}, bf16[512,256]{1,0:T(8,128)(2,1)S(1)}, u32[]{:S(2)}, u32[]{:S(2)}) collective-permute-start(bf16[512,256]{1,0:T(8,128)(2,1)S(1)} %shard_map.83.refs_1_), channel_id=1, source_target_pairs={{0,9},{1,8},{2,11},{3,10},{4,13},{5,12},{6,15},{7,14},{8,1},{9,0},... | collective-permute-start | bytes 786440 | tf_op jit(solution)/shard_map/ppermute | solution.py:170
  110.7 11.7 %collective-permute-start.11 = (bf16[512,256]{1,0:T(8,128)(2,1)S(1)}, bf16[512,256]{1,0:T(8,128)(2,1)S(1)}, u32[]{:S(2)}, u32[]{:S(2)}) collective-permute-start(bf16[512,256]{1,0:T(8,128)(2,1)S(1)} %shard_map.83.refs_1_), channel_id=1, source_target_pairs={{0,8},{1,9},{2,10},{3,11},{4,12},{5,13},{6,14},{7,15},{8,0},{9,1},... | collective-permute-start | bytes 786440 | tf_op jit(solution)/shard_map/ppermute | solution.py:170
  116.9 7.1 %collective-permute-start.9 = (bf16[512,256]{1,0:T(8,128)(2,1)S(1)}, bf16[512,256]{1,0:T(8,128)(2,1)S(1)}, u32[]{:S(2)}, u32[]{:S(2)}) collective-permute-start(bf16[512,256]{1,0:T(8,128)(2,1)S(1)} %shard_map.83.refs_1_), channel_id=1, source_target_pairs={{0,1},{1,0},{2,3},{3,2},{4,5},{5,4},{6,7},{7,6},{8,9},{9,8},{10,11... | collective-permute-start | bytes 786440 | tf_op jit(solution)/shard_map/ppermute | solution.py:170
  (3 other events, 23.8 us)

commit v2 on v1

--- a/solution.py
+++ b/solution.py
@@ -26,31 +26,63 @@
     return parts
 
 
-def attention_kernel(start_ref, lambda_ref, gain_ref, q_ref, *refs):
-    blocks, out_ref, score_ref = refs[:5], refs[5], refs[6]
+def pack_kernel(keys_ref, values_ref, out_ref, sems):
+    width = keys_ref.shape[1]
+    copies = [
+        pltpu.make_async_copy(keys_ref, out_ref.at[:, pl.ds(0, width)], sems.at[0]),
+        pltpu.make_async_copy(values_ref, out_ref.at[:, pl.ds(width, width)], sems.at[1]),
+    ]
+    for copy in copies:
+        copy.start()
+    for copy in copies:
+        copy.wait()
+
+
+def pack(keys, values):
+    whole = pl.BlockSpec(memory_space=pl.ANY)
+    return pl.pallas_call(
+        pack_kernel,
+        out_shape=jax.ShapeDtypeStruct((TOK, 8 * HD), jnp.bfloat16),
+        in_specs=[whole] * 2,
+        out_specs=whole,
+        scratch_shapes=[pltpu.SemaphoreType.DMA((2,))],
+        cost_estimate=pl.CostEstimate(flops=0, bytes_accessed=2 * MIB, transcendentals=0),
+    )(keys, values)
+
+
+def attention_kernel(
+    head, core_ref, start_ref, lambda_ref, gain_ref, q_ref, keys_ref, values_ref,
+    twin_ref, two_ref, other_ref, four_ref, out_ref, score_ref,
+):
+    width = 2 * HD
+    key_column, value_column = head * width, (2 + head) * width
+    back = [0, 1 + 2 * core_ref[0], 2, 3 - 2 * core_ref[0], 4]
+    key_refs = [keys_ref, twin_ref, two_ref, other_ref, four_ref]
+    value_refs = [values_ref] + key_refs[1:]
     factor = HD**-0.5 * math.log2(math.e)
     for tile in range(TOK // TILE):
         rows = pl.ds(tile * TILE, TILE)
         starts = start_ref[rows, :]
         ratio = []
         for which in range(2):
-            columns = slice(which * HD, (which + 1) * HD)
-            query = q_ref[rows, columns]
+            column = head * width + which * HD
+            query = q_ref[rows, column : column + HD]
             best = jnp.full((TILE, HD), NEG, jnp.float32)
             at = 0
             places = []
             for offset, low, high in segments(tile):
                 size = high - low
+                column = key_column + which * HD
                 score = (
                     lax.dot_general(
                         query,
-                        blocks[offset][low:high, columns],
+                        key_refs[offset][low:high, column : column + HD],
                         (((1,), (1,)), ((), ())),
                         preferred_element_type=jnp.float32,
                     )
                     * factor
                 )
-                key = lax.broadcasted_iota(jnp.int32, (TILE, size), 1) + (low - offset * TOK)
+                key = lax.broadcasted_iota(jnp.int32, (TILE, size), 1) + (low - back[offset] * TOK)
                 live = key >= starts
                 if offset == 0:
                     token = lax.broadcasted_iota(jnp.int32, (TILE, size), 0) + tile * TILE
@@ -63,69 +95,77 @@
                 at += size
             row_max = jnp.max(best, axis=1, keepdims=True)
             total = jnp.zeros((TILE, HD), jnp.float32)
-            summed = jnp.zeros((TILE, 2 * HD), jnp.float32)
+            summed = jnp.zeros((TILE, width), jnp.float32)
             for offset, low, high, at in places:
                 size = high - low
+                column = key_column if offset == 0 else value_column
                 weight = jnp.exp2(score_ref[:, at : at + size] - row_max)
                 for piece in range(0, size, HD):
                     total = total + weight[:, piece : piece + HD]
                 summed = summed + jnp.dot(
                     weight.astype(jnp.bfloat16),
-                    blocks[offset][low:high, 2 * HD :],
+                    value_refs[offset][low:high, column : column + width],
                     preferred_element_type=jnp.float32,
                 )
             ratio.append(summed / jnp.sum(total, axis=1, keepdims=True))
-        combined = ratio[0] - lambda_ref[0] * ratio[1]
+        combined = ratio[0] - lambda_ref[head] * ratio[1]
         power = jnp.mean(combined * combined, axis=1, keepdims=True)
         out_ref[rows, :] = (
             combined * lax.rsqrt(power + EPS) * gain_ref[...] * (1.0 - LAMBDA_INIT)
         ).astype(jnp.bfloat16)
 
 
-def attention(starts, scale, gain, query, blocks):
+def attention(head, core, starts, scale, gain, query, keys, values, blocks):
     vmem = pl.BlockSpec(memory_space=pltpu.VMEM)
-    return pl.pallas_call(
-        attention_kernel,
+    smem = pl.BlockSpec(memory_space=pltpu.SMEM)
+    return pl.pallas_call(
+        functools.partial(attention_kernel, head),
         out_shape=jax.ShapeDtypeStruct((TOK, 2 * HD), jnp.bfloat16),
-        in_specs=[vmem, pl.BlockSpec(memory_space=pltpu.SMEM)] + [vmem] * 7,
+        in_specs=[smem, vmem, smem] + [vmem] * 8,
         out_specs=vmem,
         scratch_shapes=[pltpu.VMEM((TILE, 5 * TOK), jnp.float32)],
         compiler_params=pltpu.CompilerParams(vmem_limit_bytes=24 * MIB),
         cost_estimate=pl.CostEstimate(
             flops=2 * 2 * TOK * 5 * TOK * 3 * HD, bytes_accessed=3 * MIB, transcendentals=2 * TOK * 5 * TOK
         ),
-    )(starts, scale, gain, query, *blocks)
+    )(core, starts, scale, gain, query, keys, values, *blocks)
 
 
 def project_kernel(*refs):
-    attended, weights, out_ref = refs[:8], refs[8:16], refs[16]
-    half = weights[0].shape[1]
+    attended, weights, out_ref = refs[:8], (refs[8:10], refs[10:12]), refs[12]
+    half = weights[0][0].shape[1]
     step = 256
     for side in range(2):
+        near, far = weights[side]
         for column in range(0, half, step):
             total = None
-            for member in range(4):
-                for head in range(2):
+            for head in range(2):
+                for member in range(4):
+                    first = head * 256
+                    if member == 0:
+                        weight = near[first : first + 256, column : column + step]
+                    else:
+                        first += (member - 1) * TOK
+                        weight = far[first : first + 256, column : column + step]
                     term = jnp.dot(
-                        attended[member * 2 + head][...],
-                        weights[side * 4 + member][head * 256 : (head + 1) * 256, column : column + step],
-                        preferred_element_type=jnp.float32,
+                        attended[head * 4 + member][...], weight, preferred_element_type=jnp.float32
                     )
                     total = term if total is None else total + term
-            out_ref[:, side * half + column : side * half + column + step] = total.astype(jnp.bfloat16)
+            at = side * half + column
+            out_ref[:, at : at + step] = total.astype(jnp.bfloat16)
 
 
 def project(attended, weights):
     vmem = pl.BlockSpec(memory_space=pltpu.VMEM)
-    half = weights[0].shape[1]
+    wide = 2 * weights[0].shape[1]
     return pl.pallas_call(
         project_kernel,
-        out_shape=jax.ShapeDtypeStruct((TOK, 2 * half), jnp.bfloat16),
-        in_specs=[vmem] * 16,
+        out_shape=jax.ShapeDtypeStruct((TOK, wide), jnp.bfloat16),
+        in_specs=[vmem] * 12,
         out_specs=vmem,
         compiler_params=pltpu.CompilerParams(vmem_limit_bytes=32 * MIB),
         cost_estimate=pl.CostEstimate(
-            flops=2 * TOK * 2048 * 2 * half, bytes_accessed=12 * MIB, transcendentals=0
+            flops=2 * TOK * 2048 * wide, bytes_accessed=12 * MIB, transcendentals=0
         ),
     )(*attended, *weights)
 
@@ -168,6 +208,21 @@
     high, low = divmod(member, 2)
     pairs = [(t, (((t // 8) ^ high) * 8) + ((t % 8) ^ low)) for t in range(lax.axis_size("tp"))]
     return lax.ppermute(value, "tp", pairs)
+
+
+def weight_partner(value, member):
+    high, low = divmod(member, 2)
+    count = lax.axis_size("tp")
+    pairs = []
+    for c in range(lax.axis_size("ctx")):
+        there = c ^ 2 if high and c % 2 else c
+        for t in range(count):
+            pairs.append((c * count + t, there * count + (((t // 8) ^ high) * 8) + ((t % 8) ^ low)))
+    return lax.ppermute(value, ("ctx", "tp"), pairs)
+
+
+def after(values, *results):
+    return lax.optimization_barrier((values, results))[0]
 
 
 def shards(queries, keys, values, positions, lambda_query, lambda_key, norm_gain, out_weight):
@@ -184,36 +239,30 @@
     gain = norm_gain[None, :]
     width = 2 * HD
 
-    pairs = []
-    for head in range(2):
-        part = slice(head * width, (head + 1) * width)
-        here = jnp.concatenate([keys[:, part], values[:, part]], axis=1)
-        pairs.append((here, later(here, 2), later(here, 4)))
-
+    here = pack(keys, values)
     side = out_weight.shape[1] // GROUP // 2
 
     def weight_part(member, half):
         place = (own ^ member) * (2 * side) + half * side
         return lax.dynamic_slice(out_weight, (0, place), (out_weight.shape[0], side))
 
-    mine = [weight_part(0, core)] + [partner(weight_part(d, core), d) for d in (1, 2, 3)]
-    other = [weight_part(0, 1 - core)] + [across(piece) for piece in mine[1:]]
-
-    attended = []
-    for head in range(2):
-        here, two, four = pairs[head]
-        even = core == 0
-        one, three = across((jnp.where(even, here, two), jnp.where(even, two, four)))
-        result = attention(
-            starts,
-            lambda_head[head : head + 1],
-            gain,
-            queries[:, head * width : (head + 1) * width],
-            [here, one, two, three, four],
-        )
-        attended.append([result] + [partner(result, d) for d in (1, 2, 3)])
-    flat = [attended[head][member] for member in range(4) for head in range(2)]
-    partial = project(flat, mine + other)
+    def attend(head, blocks):
+        return attention(head, core[None], starts, lambda_head, gain, queries, keys, values, blocks)
+
+    slices = [weight_part(d, core) for d in (1, 2, 3)]
+    two = later(here, 2)
+    four = later(after(here, *slices), 4)
+    mine = [weight_partner(part, d) for part, d in zip(slices, (1, 2, 3))]
+    other = across(jnp.where(core == 0, here, four))
+    blocks = [across(two), two, other, four]
+    first = attend(0, blocks)
+    gathered = [partner(first, d) for d in (1, 2, 3)]
+    second = attend(1, blocks)
+    far = jnp.concatenate(mine, axis=0)
+    swapped = across(after(far, first))
+    second, gathered[0] = after((second, gathered[0]), second)
+    both = [first, *gathered, second] + [partner(second, d) for d in (1, 2, 3)]
+    partial = project(both, [weight_part(0, core), far, weight_part(0, 1 - core), swapped])
     count = lax.axis_size("tp")
     parts = lax.all_to_all(partial.reshape(count, TOK // count, 2 * side), "tp", 0, 0)
     return total_up(core[None], parts)

time: 189 us -> 192 us (1.016)
  Pallas kernels: 20.8 us -> 51.9 us
  waiting for transfers between devices: 77.5 us -> 53.1 us
  starting transfers between devices: 21.3 us -> 17.2 us
    pallas_call x3 -> x4, Pallas kernels: 19.7 us -> 50.8 us  [the longest x1 32.9 us: pack(): pl.pallas_call(pack_kernel, out_shape=jax.ShapeDtypeStruct((TOK, 8 * HD),...]
    ppermute x9 -> x6, waiting for transfers between devices: 42.3 us -> 15.7 us  [partner(): return lax.ppermute(value, 'tp', pairs)]
    ppermute x4 -> x2, starting transfers between devices: 13.3 us -> 7.31 us  [later(): lax.ppermute(value, 'ctx', [(i, i + steps) for i in range(count - steps)])]
    ppermute x0 -> x3, starting transfers between devices: none -> 3.57 us  [weight_partner(): return lax.ppermute(value, ('ctx', 'tp'), pairs)]
    slice x3 -> x0, local copies, waits for them, and re-layouts: 2.95 us -> none  [the longest x1 1.29 us: shards(): here = jnp.concatenate([keys[:, part], values[:, part]], axis=1)]
    ppermute x0 -> x3, waiting for transfers between devices: none -> 2.75 us  [weight_partner(): return lax.ppermute(value, ('ctx', 'tp'), pairs)]
    unnamed x14 -> x16, local copies, waits for them, and re-layouts: 0.03 us -> 2.74 us
    ppermute x4 -> x2, waiting for transfers between devices: 35.2 us -> 34.7 us  [later(): lax.ppermute(value, 'ctx', [(i, i + steps) for i in range(count - steps)])]
  transfers between devices with their start and end apart: 20 -> 14, of which waited for: 10 -> 6; matrix products, arithmetic and copies ran while one was open for 5% -> 6% of each run, Pallas kernels for 7% -> 4%
where the time goes in v2:
time: 192 us; the launch traced here: 191 us
  blocking collectives  57.5 us (30%)
  waiting for transfers between devices  53.1 us (28%)
  Pallas kernels  51.9 us (27%)
  starting transfers between devices  17.2 us (9%)
  local copies, waits for them, and re-layouts  8.74 us (5%)
  other arithmetic  2.5 us (1%)
    all_to_all x1, blocking collectives, shards(): lax.all_to_all(partial.reshape(count, TOK // count, 2 * side), 'tp', 0, 0)  57.5 us
    ppermute x2, waiting for transfers between devices, later(): lax.ppermute(value, 'ctx', [(i, i + steps) for i in range(count - steps)])  34.7 us
    pallas_call x1, Pallas kernels, pack(): pl.pallas_call(pack_kernel, out_shape=jax.ShapeDtypeStruct((TOK, 8 * HD),...  32.9 us
    ppermute x6, waiting for transfers between devices, partner(): return lax.ppermute(value, 'tp', pairs)  15.7 us
    pallas_call x2, Pallas kernels, attention(): pl.pallas_call(functools.partial(attention_kernel, head), out_shape=jax.S...  13.5 us
    ppermute x2, starting transfers between devices, later(): lax.ppermute(value, 'ctx', [(i, i + steps) for i in range(count - steps)])  7.31 us
    ppermute x6, starting transfers between devices, partner(): return lax.ppermute(value, 'tp', pairs)  6.23 us
    dynamic_slice x1, local copies, waits for them, and re-layouts, weight_part(): lax.dynamic_slice(out_weight, (0, place), (out_weight.shape[0], side))  4.57 us
  transfers between devices with their start and end apart: 14, of which 6 were waited for; matrix products, arithmetic and copies ran while one was open for 6% of the time, Pallas kernels for 4%

profile of v2, /device:TPU:58, one launch (start us, length us, event | category | flops | bytes accessed | tf_op | source)
XLA Modules:
  0.0 191.3 jit_solution(2173556282733572544)
XLA Ops:
  0.0 32.9 %shard_map.82 = bf16[512,1024]{1,0:T(8,128)(2,1)} custom-call(bf16[512,512]{1,0:T(8,128)(2,1)} %keys_ref.5, bf16[512,512]{1,0:T(8,128)(2,1)} %values_ref.5), custom_call_target="tpu_custom_call" | custom-call | bytes 2097152 | tf_op jit(solution)/shard_map/pallas_call | solution.py:43
  32.9 4.1 %collective-permute-start = (bf16[512,1024]{1,0:T(8,128)(2,1)}, bf16[512,1024]{1,0:T(8,128)(2,1)}, u32[]{:S(2)}, u32[]{:S(2)}) collective-permute-start(bf16[512,1024]{1,0:T(8,128)(2,1)} %shard_map.82), channel_id=1, source_target_pairs={{0,32},{16,48},{32,64},{48,80},{64,96},{80,112},{96,128},{112,144}... | collective-permute-start | bytes 3145736 | tf_op jit(solution)/shard_map/ppermute | solution.py:200
  37.0 4.6 %constant_dynamic-slice_fusion = (bf16[512,1024]{1,0:T(8,128)(2,1)S(1)}, bf16[512,1024]{1,0:T(8,128)(2,1)}, bf16[512,1024]{1,0:T(8,128)(2,1)}, bf16[512,1024]{1,0:T(8,128)(2,1)}, bf16[512,1024]{1,0:T(8,128)(2,1)S(1)}) fusion(bf16[512,8192]{1,0:T(8,128)(2,1)} %param.15, s32[]{:T(128)S(6)} %select_n.35, s32[]{:T(128)S(6)} %select_n.32, s32[]{:T(128)S(6)} %select_n.31, ...), kind=kLoop, calls=%fused_computation.5 | loop fusion | bytes 10485780 | tf_op jit(solution)/shard_map/dynamic_slice | solution.py:247
  41.6 3.2 %collective-permute-start.2 = (bf16[512,1024]{1,0:T(8,128)(2,1)}, bf16[512,1024]{1,0:T(8,128)(2,1)S(1)}, u32[]{:S(2)}, u32[]{:S(2)}) collective-permute-start(bf16[512,1024]{1,0:T(8,128)(2,1)} %shard_map.82), channel_id=1, source_target_pairs={{0,64},{16,80},{32,96},{48,112},{64,128},{80,144},{96,160},{112,17... | collective-permute-start | bytes 3145736 | tf_op jit(solution)/shard_map/ppermute | solution.py:200
  45.0 1.2 collective-permute-start.12
  46.2 2.2 %collective-permute-start.11 = (bf16[512,1024]{1,0:T(8,128)(2,1)}, bf16[512,1024]{1,0:T(8,128)(2,1)}, u32[]{:S(2)}, u32[]{:S(2)}) collective-permute-start(bf16[512,1024]{1,0:T(8,128)(2,1)} %get-tuple-element.17), channel_id=1, source_target_pairs={{0,8},{1,9},{2,10},{3,11},{4,12},{5,13},{6,14},{7,15},{8,0},{9,1},... | collective-permute-start | bytes 3145736 | tf_op jit(solution)/shard_map/ppermute | solution.py:221
  48.4 13.2 %collective-permute-done.two_ref = bf16[512,1024]{1,0:T(8,128)(2,1)} collective-permute-done((bf16[512,1024]{1,0:T(8,128)(2,1)}, bf16[512,1024]{1,0:T(8,128)(2,1)}, u32[]{:S(2)}, u32[]{:S(2)}) %collective-permute-start) | collective-permute-done | bytes 1048608 | tf_op jit(solution)/shard_map/ppermute | solution.py:200
  61.6 21.5 %collective-permute-done.2.four_ref = bf16[512,1024]{1,0:T(8,128)(2,1)S(1)} collective-permute-done((bf16[512,1024]{1,0:T(8,128)(2,1)}, bf16[512,1024]{1,0:T(8,128)(2,1)S(1)}, u32[]{:S(2)}, u32[]{:S(2)}) %collective-permute-start.2) | collective-permute-done | bytes 1048608 | tf_op jit(solution)/shard_map/ppermute | solution.py:200
  83.1 2.3 %broadcast_select_fusion = bf16[512,1024]{1,0:T(8,128)(2,1)} fusion(bf16[512,1024]{1,0:T(8,128)(2,1)} %shard_map.82, bf16[512,1024]{1,0:T(8,128)(2,1)S(1)} %collective-permute-done.2.four_ref, pred[]{:T(512)S(6)} %eq.3), kind=kLoop, calls=%fused_computation | loop fusion | flops 524288 | bytes 3145729 | tf_op jit(solution)/shard_map/jit(_where)/select_n | solution.py:256
  85.9 1.4 constant_dynamic-update-slice_fusion.2
  87.3 1.3 constant_dynamic-update-slice_fusion.1
  88.6 2.7 %collective-permute-done.12 = bf16[512,1024]{1,0:T(8,128)(2,1)} collective-permute-done((bf16[512,1024]{1,0:T(8,128)(2,1)}, bf16[512,1024]{1,0:T(8,128)(2,1)}, u32[]{:S(2)}, u32[]{:S(2)}) %collective-permute-start.12) | collective-permute-done | bytes 1048608 | tf_op jit(solution)/shard_map/ppermute | solution.py:221
  91.3 1.3 constant_dynamic-update-slice_fusion.refs_9_
  92.7 6.7 %shard_map.83.refs_0_ = bf16[512,256]{1,0:T(8,128)(2,1)S(1)} custom-call(s32[1]{0:T(128)} %bitcast.core_ref, s32[512,1]{1,0:T(8,128)S(1)} %copy.9.start_ref, f32[2]{0:T(128)S(1)} %subtract_add_fusion.lambda_ref, f32[1,256]{1,0:T(1,128)S(1)} %bitcast.5, bf16[512,512]{1,0:T(8,128)(2,1)S(1)} %copy-done.2, bf16[512,512]{1,0:T(8,128)(2,1)S(1)} %copy-done, ...), custom_call_target="tpu_custom_call" | custom-call | flops 2013265920 | bytes 3145728 | tf_op jit(solution)/shard_map/pallas_call | solution.py:121
  99.9 3.4 %collective-permute-start.6 = (bf16[512,256]{1,0:T(8,128)(2,1)S(1)}, bf16[512,256]{1,0:T(8,128)(2,1)S(1)}, u32[]{:S(2)}, u32[]{:S(2)}) collective-permute-start(bf16[512,256]{1,0:T(8,128)(2,1)S(1)} %shard_map.83.refs_0_), channel_id=1, source_target_pairs={{0,9},{1,8},{2,11},{3,10},{4,13},{5,12},{6,15},{7,14},{8,1},{9,0},... | collective-permute-start | bytes 786440 | tf_op jit(solution)/shard_map/ppermute | solution.py:210
  103.3 6.7 %shard_map.84.refs_4_ = bf16[512,256]{1,0:T(8,128)(2,1)S(1)} custom-call(s32[1]{0:T(128)} %bitcast.core_ref, s32[512,1]{1,0:T(8,128)S(1)} %copy.9.start_ref, f32[2]{0:T(128)S(1)} %subtract_add_fusion.lambda_ref, f32[1,256]{1,0:T(1,128)S(1)} %bitcast.6, bf16[512,512]{1,0:T(8,128)(2,1)S(1)} %copy-done.2, bf16[512,512]{1,0:T(8,128)(2,1)S(1)} %copy-done, ...), custom_call_target="tpu_custom_call" | custom-call | flops 2013265920 | bytes 3145728 | tf_op jit(solution)/shard_map/pallas_call | solution.py:121
  110.0 1.8 collective-permute-start.9
  111.8 0.4 collective-permute-start.8
  112.2 3.8 %collective-permute-done.6.refs_3_ = bf16[512,256]{1,0:T(8,128)(2,1)S(1)} collective-permute-done((bf16[512,256]{1,0:T(8,128)(2,1)S(1)}, bf16[512,256]{1,0:T(8,128)(2,1)S(1)}, u32[]{:S(2)}, u32[]{:S(2)}) %collective-permute-start.6) | collective-permute-done | bytes 262176 | tf_op jit(solution)/shard_map/ppermute | solution.py:210
  116.4 7.3 %collective-permute-done.5.refs_2_ = bf16[512,256]{1,0:T(8,128)(2,1)S(1)} collective-permute-done((bf16[512,256]{1,0:T(8,128)(2,1)S(1)}, bf16[512,256]{1,0:T(8,128)(2,1)S(1)}, u32[]{:S(2)}, u32[]{:S(2)}) %collective-permute-start.5) | collective-permute-done | bytes 262176 | tf_op jit(solution)/shard_map/ppermute | solution.py:210
  123.7 4.5 %collective-permute-done.8.refs_6_ = bf16[512,256]{1,0:T(8,128)(2,1)S(1)} collective-permute-done((bf16[512,256]{1,0:T(8,128)(2,1)S(1)}, bf16[512,256]{1,0:T(8,128)(2,1)S(1)}, u32[]{:S(2)}, u32[]{:S(2)}) %collective-permute-start.8) | collective-permute-done | bytes 262176 | tf_op jit(solution)/shard_map/ppermute | solution.py:210
  128.2 4.5 %shard_map.85 = bf16[512,2048]{1,0:T(8,128)(2,1)S(1)} custom-call(bf16[512,256]{1,0:T(8,128)(2,1)S(1)} %shard_map.83.refs_0_, bf16[512,256]{1,0:T(8,128)(2,1)S(1)} %collective-permute-done.4.refs_1_, bf16[512,256]{1,0:T(8,128)(2,1)S(1)} %collective-permute-done.5.refs_2_, bf16[512,256]{1,0:T(8,128)(2,1)S(1)} %collective-permute-done.6.refs_3_, ...), custom_call_target="tpu_custom_call" | custom-call | flops 4294967296 | bytes 12582912 | tf_op jit(solution)/shard_map/pallas_call | solution.py:161
  132.7 57.5 %all_to_all.5.parts_ref = bf16[16,32,2048]{2,1,0:T(8,128)(2,1)S(1)} all-to-all(bf16[16,32,2048]{2,1,0:T(8,128)(2,1)S(1)} %bitcast.4), channel_id=1, replica_groups=mesh['ctx'=16,'tp'=16] {'tp'}, dimensions={0} | all-to-all | bytes 4194304 | tf_op jit(solution)/shard_map/all_to_all | solution.py:267
  190.2 1.0 shard_map.86
  (33 shorter events, 1.3 us)
Async XLA Ops:
  32.9 28.7 %collective-permute-start = (bf16[512,1024]{1,0:T(8,128)(2,1)}, bf16[512,1024]{1,0:T(8,128)(2,1)}, u32[]{:S(2)}, u32[]{:S(2)}) collective-permute-start(bf16[512,1024]{1,0:T(8,128)(2,1)} %shard_map.82), channel_id=1, source_target_pairs={{0,32},{16,48},{32,64},{48,80},{64,96},{80,112},{96,128},{112,144}... | collective-permute-start | bytes 3145736 | tf_op jit(solution)/shard_map/ppermute | solution.py:200
  41.6 43.9 %copy-start.4 = (s32[512]{0:T(512)S(1)}, s32[512]{0:T(512)}, u32[]{:S(2)}) copy-start(s32[512]{0:T(512)} %param.11) | copy-start | bytes 6148
  41.6 44.1 %copy-start.5 = (f32[2,256]{1,0:T(2,128)S(1)}, f32[2,256]{1,0:T(2,128)}, u32[]{:S(2)}) copy-start(f32[2,256]{1,0:T(2,128)} %param.13) | copy-start | bytes 6148
  41.6 44.1 %copy-start.6 = (f32[2,256]{1,0:T(2,128)S(1)}, f32[2,256]{1,0:T(2,128)}, u32[]{:S(2)}) copy-start(f32[2,256]{1,0:T(2,128)} %param.12) | copy-start | bytes 6148
  41.6 41.5 %collective-permute-start.2 = (bf16[512,1024]{1,0:T(8,128)(2,1)}, bf16[512,1024]{1,0:T(8,128)(2,1)S(1)}, u32[]{:S(2)}, u32[]{:S(2)}) collective-permute-start(bf16[512,1024]{1,0:T(8,128)(2,1)} %shard_map.82), channel_id=1, source_target_pairs={{0,64},{16,80},{32,96},{48,112},{64,128},{80,144},{96,160},{112,17... | collective-permute-start | bytes 3145736 | tf_op jit(solution)/shard_map/ppermute | solution.py:200
  44.8 41.0 %collective-permute-start.10 = (bf16[512,1024]{1,0:T(8,128)(2,1)}, bf16[512,1024]{1,0:T(8,128)(2,1)}, u32[]{:S(2)}, u32[]{:S(2)}) collective-permute-start(bf16[512,1024]{1,0:T(8,128)(2,1)} %get-tuple-element.18), channel_id=1, source_target_pairs={{0,1},{1,0},{2,3},{3,2},{4,5},{5,4},{6,7},{7,6},{8,9},{9,8},{10,11... | collective-permute-start | bytes 3145736 | tf_op jit(solution)/shard_map/ppermute | solution.py:221
  45.0 46.3 %collective-permute-start.12 = (bf16[512,1024]{1,0:T(8,128)(2,1)}, bf16[512,1024]{1,0:T(8,128)(2,1)}, u32[]{:S(2)}, u32[]{:S(2)}) collective-permute-start(bf16[512,1024]{1,0:T(8,128)(2,1)} %get-tuple-element.16), channel_id=1, source_target_pairs={{0,9},{1,8},{2,11},{3,10},{4,13},{5,12},{6,15},{7,14},{8,1},{9,0},... | collective-permute-start | bytes 3145736 | tf_op jit(solution)/shard_map/ppermute | solution.py:221
  46.2 41.1 %collective-permute-start.11 = (bf16[512,1024]{1,0:T(8,128)(2,1)}, bf16[512,1024]{1,0:T(8,128)(2,1)}, u32[]{:S(2)}, u32[]{:S(2)}) collective-permute-start(bf16[512,1024]{1,0:T(8,128)(2,1)} %get-tuple-element.17), channel_id=1, source_target_pairs={{0,8},{1,9},{2,10},{3,11},{4,12},{5,13},{6,14},{7,15},{8,0},{9,1},... | collective-permute-start | bytes 3145736 | tf_op jit(solution)/shard_map/ppermute | solution.py:221
  61.6 31.0 %collective-permute-start.1 = (bf16[512,1024]{1,0:T(8,128)(2,1)}, bf16[512,1024]{1,0:T(8,128)(2,1)}, u32[]{:S(2)}, u32[]{:S(2)}) collective-permute-start(bf16[512,1024]{1,0:T(8,128)(2,1)} %collective-permute-done.two_ref), channel_id=1, source_target_pairs={{0,16},{16,0},{32,48},{48,32},{64,80},{80,64},{96,112},{112,96},{1... | collective-permute-start | bytes 3145736 | tf_op jit(solution)/shard_map/ppermute | solution.py:204
  85.5 7.2 %collective-permute-start.3 = (bf16[512,1024]{1,0:T(8,128)(2,1)}, bf16[512,1024]{1,0:T(8,128)(2,1)}, u32[]{:S(2)}, u32[]{:S(2)}) collective-permute-start(bf16[512,1024]{1,0:T(8,128)(2,1)} %broadcast_select_fusion), channel_id=1, source_target_pairs={{0,16},{16,0},{32,48},{48,32},{64,80},{80,64},{96,112},{112,96},{1... | collective-permute-start | bytes 3145736 | tf_op jit(solution)/shard_map/ppermute | solution.py:204
  85.8 6.8 %copy-start = (bf16[512,512]{1,0:T(8,128)(2,1)S(1)}, bf16[512,512]{1,0:T(8,128)(2,1)}, u32[]{:S(2)}) copy-start(bf16[512,512]{1,0:T(8,128)(2,1)} %keys_ref.5) | copy-start | bytes 1572868
  85.8 6.8 %copy-start.1 = (bf16[512,512]{1,0:T(8,128)(2,1)S(1)}, bf16[512,512]{1,0:T(8,128)(2,1)}, u32[]{:S(2)}) copy-start(bf16[512,512]{1,0:T(8,128)(2,1)} %values_ref.5) | copy-start | bytes 1572868
  85.8 6.8 %copy-start.2 = (bf16[512,512]{1,0:T(8,128)(2,1)S(1)}, bf16[512,512]{1,0:T(8,128)(2,1)}, u32[]{:S(2)}) copy-start(bf16[512,512]{1,0:T(8,128)(2,1)} %q_ref.3) | copy-start | bytes 1572868
  85.9 6.8 %copy-start.3 = (f32[256]{0:T(256)S(1)}, f32[256]{0:T(256)}, u32[]{:S(2)}) copy-start(f32[256]{0:T(256)} %param.14) | copy-start | bytes 3076
  99.4 28.8 %collective-permute-start.13 = (bf16[1536,1024]{1,0:T(8,128)(2,1)S(1)}, bf16[1536,1024]{1,0:T(8,128)(2,1)S(1)}, u32[]{:S(2)}, u32[]{:S(2)}) collective-permute-start(bf16[1536,1024]{1,0:T(8,128)(2,1)S(1)} %constant_dynamic-update-slice_fusion.refs_9_), channel_id=1, source_target_pairs={{0,16},{16,0},{32,48},{48,32},{64,80},{80,64},{96,112},{112,96},{1... | collective-permute-start | bytes 9437192 | tf_op jit(solution)/shard_map/ppermute | solution.py:204
  99.5 10.5 %collective-permute-start.4 = (bf16[512,256]{1,0:T(8,128)(2,1)S(1)}, bf16[512,256]{1,0:T(8,128)(2,1)S(1)}, u32[]{:S(2)}, u32[]{:S(2)}) collective-permute-start(bf16[512,256]{1,0:T(8,128)(2,1)S(1)} %shard_map.83.refs_0_), channel_id=1, source_target_pairs={{0,1},{1,0},{2,3},{3,2},{4,5},{5,4},{6,7},{7,6},{8,9},{9,8},{10,11... | collective-permute-start | bytes 786440 | tf_op jit(solution)/shard_map/ppermute | solution.py:210
  99.9 16.2 %collective-permute-start.6 = (bf16[512,256]{1,0:T(8,128)(2,1)S(1)}, bf16[512,256]{1,0:T(8,128)(2,1)S(1)}, u32[]{:S(2)}, u32[]{:S(2)}) collective-permute-start(bf16[512,256]{1,0:T(8,128)(2,1)S(1)} %shard_map.83.refs_0_), channel_id=1, source_target_pairs={{0,9},{1,8},{2,11},{3,10},{4,13},{5,12},{6,15},{7,14},{8,1},{9,0},... | collective-permute-start | bytes 786440 | tf_op jit(solution)/shard_map/ppermute | solution.py:210
  103.3 20.4 %collective-permute-start.5 = (bf16[512,256]{1,0:T(8,128)(2,1)S(1)}, bf16[512,256]{1,0:T(8,128)(2,1)S(1)}, u32[]{:S(2)}, u32[]{:S(2)}) collective-permute-start(bf16[512,256]{1,0:T(8,128)(2,1)S(1)} %shard_map.83.refs_0_), channel_id=1, source_target_pairs={{0,8},{1,9},{2,10},{3,11},{4,12},{5,13},{6,14},{7,15},{8,0},{9,1},... | collective-permute-start | bytes 786440 | tf_op jit(solution)/shard_map/ppermute | solution.py:210
  110.0 13.7 %collective-permute-start.9 = (bf16[512,256]{1,0:T(8,128)(2,1)S(1)}, bf16[512,256]{1,0:T(8,128)(2,1)S(1)}, u32[]{:S(2)}, u32[]{:S(2)}) collective-permute-start(bf16[512,256]{1,0:T(8,128)(2,1)S(1)} %shard_map.84.refs_4_), channel_id=1, source_target_pairs={{0,9},{1,8},{2,11},{3,10},{4,13},{5,12},{6,15},{7,14},{8,1},{9,0},... | collective-permute-start | bytes 786440 | tf_op jit(solution)/shard_map/ppermute | solution.py:210
  111.8 16.4 %collective-permute-start.8 = (bf16[512,256]{1,0:T(8,128)(2,1)S(1)}, bf16[512,256]{1,0:T(8,128)(2,1)S(1)}, u32[]{:S(2)}, u32[]{:S(2)}) collective-permute-start(bf16[512,256]{1,0:T(8,128)(2,1)S(1)} %shard_map.84.refs_4_), channel_id=1, source_target_pairs={{0,8},{1,9},{2,10},{3,11},{4,12},{5,13},{6,14},{7,15},{8,0},{9,1},... | collective-permute-start | bytes 786440 | tf_op jit(solution)/shard_map/ppermute | solution.py:210
  116.1 12.1 %collective-permute-start.7 = (bf16[512,256]{1,0:T(8,128)(2,1)S(1)}, bf16[512,256]{1,0:T(8,128)(2,1)S(1)}, u32[]{:S(2)}, u32[]{:S(2)}) collective-permute-start(bf16[512,256]{1,0:T(8,128)(2,1)S(1)} %shard_map.84.refs_4_), channel_id=1, source_target_pairs={{0,1},{1,0},{2,3},{3,2},{4,5},{5,4},{6,7},{7,6},{8,9},{9,8},{10,11... | collective-permute-start | bytes 786440 | tf_op jit(solution)/shard_map/ppermute | solution.py:210

commit v3 on v2

--- a/solution.py
+++ b/solution.py
@@ -239,7 +239,7 @@
     gain = norm_gain[None, :]
     width = 2 * HD
 
-    here = pack(keys, values)
+    here = jnp.concatenate([keys, values], axis=1)
     side = out_weight.shape[1] // GROUP // 2
 
     def weight_part(member, half):

time: 192 us -> 163 us (0.85)
  Pallas kernels: 51.9 us -> 19 us
  local copies, waits for them, and re-layouts: 8.74 us -> 12.6 us
    pallas_call x1 -> x0, Pallas kernels: 32.9 us -> none  [pack(): pl.pallas_call(pack_kernel, out_shape=jax.ShapeDtypeStruct((TOK, 8 * HD),...]
    concatenate x0 -> x1, local copies, waits for them, and re-layouts: none -> 1.96 us  [shards(): here = jnp.concatenate([keys, values], axis=1)]
    unnamed x16 -> x17, local copies, waits for them, and re-layouts: 2.74 us -> 4.69 us
  transfers between devices with their start and end apart: 14 -> 14, of which waited for: 6 -> 6; matrix products, arithmetic and copies ran while one was open for 6% -> 7% of each run, Pallas kernels for 4% -> 4%
where the time goes in v3:
time: 163 us; the launch traced here: 162 us
  blocking collectives  57.5 us (35%)
  waiting for transfers between devices  53.1 us (33%)
  Pallas kernels  19 us (12%)
  starting transfers between devices  17.2 us (11%)
  local copies, waits for them, and re-layouts  12.6 us (8%)
  other arithmetic  2.53 us (2%)
    all_to_all x1, blocking collectives, shards(): lax.all_to_all(partial.reshape(count, TOK // count, 2 * side), 'tp', 0, 0)  57.5 us
    ppermute x2, waiting for transfers between devices, later(): lax.ppermute(value, 'ctx', [(i, i + steps) for i in range(count - steps)])  34.8 us
    ppermute x6, waiting for transfers between devices, partner(): return lax.ppermute(value, 'tp', pairs)  15.7 us
    pallas_call x2, Pallas kernels, attention(): pl.pallas_call(functools.partial(attention_kernel, head), out_shape=jax.S...  13.5 us
    ppermute x2, starting transfers between devices, later(): lax.ppermute(value, 'ctx', [(i, i + steps) for i in range(count - steps)])  7.3 us
    ppermute x6, starting transfers between devices, partner(): return lax.ppermute(value, 'tp', pairs)  6.23 us
    unnamed x17, local copies, waits for them, and re-layouts  4.69 us
    pallas_call x1, Pallas kernels, project(): pl.pallas_call(project_kernel, out_shape=jax.ShapeDtypeStruct((TOK, wide)...  4.49 us
  transfers between devices with their start and end apart: 14, of which 6 were waited for; matrix products, arithmetic and copies ran while one was open for 7% of the time, Pallas kernels for 4%

profile of v3, /device:TPU:58, one launch (start us, length us, event | category | flops | bytes accessed | tf_op | source)
XLA Modules:
  0.0 162.2 jit_solution(4940569365296981465)
XLA Ops:
  0.0 1.9 %constant_dynamic-update-slice_fusion.1 = bf16[512,1024]{1,0:T(8,128)(2,1)} fusion(bf16[512,512]{1,0:T(8,128)(2,1)} %keys_ref.3), kind=kLoop, calls=%fused_computation.2 | loop fusion | bytes 1048576
  2.0 2.0 %constant_dynamic-update-slice_fusion = bf16[512,1024]{1,0:T(8,128)(2,1)} fusion(bf16[512,1024]{1,0:T(8,128)(2,1)} %constant_dynamic-update-slice_fusion.1, bf16[512,512]{1,0:T(8,128)(2,1)} %values_ref.3), kind=kLoop, calls=%fused_computation.1 | loop fusion | bytes 1048576 | tf_op jit(solution)/shard_map/concatenate | solution.py:242
  3.9 4.1 %collective-permute-start = (bf16[512,1024]{1,0:T(8,128)(2,1)}, bf16[512,1024]{1,0:T(8,128)(2,1)}, u32[]{:S(2)}, u32[]{:S(2)}) collective-permute-start(bf16[512,1024]{1,0:T(8,128)(2,1)} %constant_dynamic-update-slice_fusion), channel_id=1, source_target_pairs={{0,32},{16,48},{32,64},{48,80},{64,96},{80,112},{96,128},{112,144}... | collective-permute-start | bytes 3145736 | tf_op jit(solution)/shard_map/ppermute | solution.py:200
  8.0 4.5 %constant_dynamic-slice_fusion = (bf16[512,1024]{1,0:T(8,128)(2,1)S(1)}, bf16[512,1024]{1,0:T(8,128)(2,1)}, bf16[512,1024]{1,0:T(8,128)(2,1)}, bf16[512,1024]{1,0:T(8,128)(2,1)}, bf16[512,1024]{1,0:T(8,128)(2,1)S(1)}) fusion(bf16[512,8192]{1,0:T(8,128)(2,1)} %param.15, s32[]{:T(128)S(6)} %select_n.35, s32[]{:T(128)S(6)} %select_n.32, s32[]{:T(128)S(6)} %select_n.31, ...), kind=kLoop, calls=%fused_computation.7 | loop fusion | bytes 10485780 | tf_op jit(solution)/shard_map/dynamic_slice | solution.py:247
  12.5 3.2 %collective-permute-start.2 = (bf16[512,1024]{1,0:T(8,128)(2,1)}, bf16[512,1024]{1,0:T(8,128)(2,1)S(1)}, u32[]{:S(2)}, u32[]{:S(2)}) collective-permute-start(bf16[512,1024]{1,0:T(8,128)(2,1)} %constant_dynamic-update-slice_fusion), channel_id=1, source_target_pairs={{0,64},{16,80},{32,96},{48,112},{64,128},{80,144},{96,160},{112,17... | collective-permute-start | bytes 3145736 | tf_op jit(solution)/shard_map/ppermute | solution.py:200
  15.9 1.2 collective-permute-start.12
  17.1 2.2 %collective-permute-start.11 = (bf16[512,1024]{1,0:T(8,128)(2,1)}, bf16[512,1024]{1,0:T(8,128)(2,1)}, u32[]{:S(2)}, u32[]{:S(2)}) collective-permute-start(bf16[512,1024]{1,0:T(8,128)(2,1)} %get-tuple-element.17), channel_id=1, source_target_pairs={{0,8},{1,9},{2,10},{3,11},{4,12},{5,13},{6,14},{7,15},{8,0},{9,1},... | collective-permute-start | bytes 3145736 | tf_op jit(solution)/shard_map/ppermute | solution.py:221
  19.3 13.3 %collective-permute-done.two_ref = bf16[512,1024]{1,0:T(8,128)(2,1)} collective-permute-done((bf16[512,1024]{1,0:T(8,128)(2,1)}, bf16[512,1024]{1,0:T(8,128)(2,1)}, u32[]{:S(2)}, u32[]{:S(2)}) %collective-permute-start) | collective-permute-done | bytes 1048608 | tf_op jit(solution)/shard_map/ppermute | solution.py:200
  32.6 21.5 %collective-permute-done.2.four_ref = bf16[512,1024]{1,0:T(8,128)(2,1)S(1)} collective-permute-done((bf16[512,1024]{1,0:T(8,128)(2,1)}, bf16[512,1024]{1,0:T(8,128)(2,1)S(1)}, u32[]{:S(2)}, u32[]{:S(2)}) %collective-permute-start.2) | collective-permute-done | bytes 1048608 | tf_op jit(solution)/shard_map/ppermute | solution.py:200
  54.1 2.4 %broadcast_select_fusion = bf16[512,1024]{1,0:T(8,128)(2,1)} fusion(bf16[512,1024]{1,0:T(8,128)(2,1)} %constant_dynamic-update-slice_fusion, bf16[512,1024]{1,0:T(8,128)(2,1)S(1)} %collective-permute-done.2.four_ref, pred[]{:T(512)S(6)} %eq.3), kind=kLoop, calls=%fused_computation | loop fusion | flops 524288 | bytes 3145729 | tf_op jit(solution)/shard_map/jit(_where)/select_n | solution.py:256
  56.9 1.4 constant_dynamic-update-slice_fusion.4
  58.3 1.3 constant_dynamic-update-slice_fusion.3
  59.6 2.6 %collective-permute-done.12 = bf16[512,1024]{1,0:T(8,128)(2,1)} collective-permute-done((bf16[512,1024]{1,0:T(8,128)(2,1)}, bf16[512,1024]{1,0:T(8,128)(2,1)}, u32[]{:S(2)}, u32[]{:S(2)}) %collective-permute-start.12) | collective-permute-done | bytes 1048608 | tf_op jit(solution)/shard_map/ppermute | solution.py:221
  62.2 1.3 constant_dynamic-update-slice_fusion.2.refs_9_
  63.6 6.7 %shard_map.82.refs_0_ = bf16[512,256]{1,0:T(8,128)(2,1)S(1)} custom-call(s32[1]{0:T(128)} %bitcast.core_ref, s32[512,1]{1,0:T(8,128)S(1)} %copy.9.start_ref, f32[2]{0:T(128)S(1)} %subtract_add_fusion.lambda_ref, f32[1,256]{1,0:T(1,128)S(1)} %bitcast.5, bf16[512,512]{1,0:T(8,128)(2,1)S(1)} %copy-done.2, bf16[512,512]{1,0:T(8,128)(2,1)S(1)} %copy-done, ...), custom_call_target="tpu_custom_call" | custom-call | flops 2013265920 | bytes 3145728 | tf_op jit(solution)/shard_map/pallas_call | solution.py:121
  70.8 3.4 %collective-permute-start.6 = (bf16[512,256]{1,0:T(8,128)(2,1)S(1)}, bf16[512,256]{1,0:T(8,128)(2,1)S(1)}, u32[]{:S(2)}, u32[]{:S(2)}) collective-permute-start(bf16[512,256]{1,0:T(8,128)(2,1)S(1)} %shard_map.82.refs_0_), channel_id=1, source_target_pairs={{0,9},{1,8},{2,11},{3,10},{4,13},{5,12},{6,15},{7,14},{8,1},{9,0},... | collective-permute-start | bytes 786440 | tf_op jit(solution)/shard_map/ppermute | solution.py:210
  74.2 6.7 %shard_map.83.refs_4_ = bf16[512,256]{1,0:T(8,128)(2,1)S(1)} custom-call(s32[1]{0:T(128)} %bitcast.core_ref, s32[512,1]{1,0:T(8,128)S(1)} %copy.9.start_ref, f32[2]{0:T(128)S(1)} %subtract_add_fusion.lambda_ref, f32[1,256]{1,0:T(1,128)S(1)} %bitcast.6, bf16[512,512]{1,0:T(8,128)(2,1)S(1)} %copy-done.2, bf16[512,512]{1,0:T(8,128)(2,1)S(1)} %copy-done, ...), custom_call_target="tpu_custom_call" | custom-call | flops 2013265920 | bytes 3145728 | tf_op jit(solution)/shard_map/pallas_call | solution.py:121
  80.9 1.8 %collective-permute-start.9 = (bf16[512,256]{1,0:T(8,128)(2,1)S(1)}, bf16[512,256]{1,0:T(8,128)(2,1)S(1)}, u32[]{:S(2)}, u32[]{:S(2)}) collective-permute-start(bf16[512,256]{1,0:T(8,128)(2,1)S(1)} %shard_map.83.refs_4_), channel_id=1, source_target_pairs={{0,9},{1,8},{2,11},{3,10},{4,13},{5,12},{6,15},{7,14},{8,1},{9,0},... | collective-permute-start | bytes 786440 | tf_op jit(solution)/shard_map/ppermute | solution.py:210
  83.1 3.8 %collective-permute-done.6.refs_3_ = bf16[512,256]{1,0:T(8,128)(2,1)S(1)} collective-permute-done((bf16[512,256]{1,0:T(8,128)(2,1)S(1)}, bf16[512,256]{1,0:T(8,128)(2,1)S(1)}, u32[]{:S(2)}, u32[]{:S(2)}) %collective-permute-start.6) | collective-permute-done | bytes 262176 | tf_op jit(solution)/shard_map/ppermute | solution.py:210
  87.3 7.3 %collective-permute-done.5.refs_2_ = bf16[512,256]{1,0:T(8,128)(2,1)S(1)} collective-permute-done((bf16[512,256]{1,0:T(8,128)(2,1)S(1)}, bf16[512,256]{1,0:T(8,128)(2,1)S(1)}, u32[]{:S(2)}, u32[]{:S(2)}) %collective-permute-start.5) | collective-permute-done | bytes 262176 | tf_op jit(solution)/shard_map/ppermute | solution.py:210
  94.6 4.5 %collective-permute-done.8.refs_6_ = bf16[512,256]{1,0:T(8,128)(2,1)S(1)} collective-permute-done((bf16[512,256]{1,0:T(8,128)(2,1)S(1)}, bf16[512,256]{1,0:T(8,128)(2,1)S(1)}, u32[]{:S(2)}, u32[]{:S(2)}) %collective-permute-start.8) | collective-permute-done | bytes 262176 | tf_op jit(solution)/shard_map/ppermute | solution.py:210
  99.1 4.5 %shard_map.84 = bf16[512,2048]{1,0:T(8,128)(2,1)S(1)} custom-call(bf16[512,256]{1,0:T(8,128)(2,1)S(1)} %shard_map.82.refs_0_, bf16[512,256]{1,0:T(8,128)(2,1)S(1)} %collective-permute-done.4.refs_1_, bf16[512,256]{1,0:T(8,128)(2,1)S(1)} %collective-permute-done.5.refs_2_, bf16[512,256]{1,0:T(8,128)(2,1)S(1)} %collective-permute-done.6.refs_3_, ...), custom_call_target="tpu_custom_call" | custom-call | flops 4294967296 | bytes 12582912 | tf_op jit(solution)/shard_map/pallas_call | solution.py:161
  103.6 57.5 %all_to_all.5.parts_ref = bf16[16,32,2048]{2,1,0:T(8,128)(2,1)S(1)} all-to-all(bf16[16,32,2048]{2,1,0:T(8,128)(2,1)S(1)} %bitcast.4), channel_id=1, replica_groups=mesh['ctx'=16,'tp'=16] {'tp'}, dimensions={0} | all-to-all | bytes 4194304 | tf_op jit(solution)/shard_map/all_to_all | solution.py:267
  161.1 1.0 shard_map.85
  (34 shorter events, 1.7 us)
Async XLA Ops:
  3.9 28.7 %collective-permute-start = (bf16[512,1024]{1,0:T(8,128)(2,1)}, bf16[512,1024]{1,0:T(8,128)(2,1)}, u32[]{:S(2)}, u32[]{:S(2)}) collective-permute-start(bf16[512,1024]{1,0:T(8,128)(2,1)} %constant_dynamic-update-slice_fusion), channel_id=1, source_target_pairs={{0,32},{16,48},{32,64},{48,80},{64,96},{80,112},{96,128},{112,144}... | collective-permute-start | bytes 3145736 | tf_op jit(solution)/shard_map/ppermute | solution.py:200
  12.5 44.0 %copy-start.4 = (s32[512]{0:T(512)S(1)}, s32[512]{0:T(512)}, u32[]{:S(2)}) copy-start(s32[512]{0:T(512)} %param.11) | copy-start | bytes 6148
  12.5 44.2 %copy-start.5 = (f32[2,256]{1,0:T(2,128)S(1)}, f32[2,256]{1,0:T(2,128)}, u32[]{:S(2)}) copy-start(f32[2,256]{1,0:T(2,128)} %param.13) | copy-start | bytes 6148
  12.5 44.2 %copy-start.6 = (f32[2,256]{1,0:T(2,128)S(1)}, f32[2,256]{1,0:T(2,128)}, u32[]{:S(2)}) copy-start(f32[2,256]{1,0:T(2,128)} %param.12) | copy-start | bytes 6148
  12.5 41.6 %collective-permute-start.2 = (bf16[512,1024]{1,0:T(8,128)(2,1)}, bf16[512,1024]{1,0:T(8,128)(2,1)S(1)}, u32[]{:S(2)}, u32[]{:S(2)}) collective-permute-start(bf16[512,1024]{1,0:T(8,128)(2,1)} %constant_dynamic-update-slice_fusion), channel_id=1, source_target_pairs={{0,64},{16,80},{32,96},{48,112},{64,128},{80,144},{96,160},{112,17... | collective-permute-start | bytes 3145736 | tf_op jit(solution)/shard_map/ppermute | solution.py:200
  15.7 41.2 %collective-permute-start.10 = (bf16[512,1024]{1,0:T(8,128)(2,1)}, bf16[512,1024]{1,0:T(8,128)(2,1)}, u32[]{:S(2)}, u32[]{:S(2)}) collective-permute-start(bf16[512,1024]{1,0:T(8,128)(2,1)} %get-tuple-element.18), channel_id=1, source_target_pairs={{0,1},{1,0},{2,3},{3,2},{4,5},{5,4},{6,7},{7,6},{8,9},{9,8},{10,11... | collective-permute-start | bytes 3145736 | tf_op jit(solution)/shard_map/ppermute | solution.py:221
  15.9 46.3 %collective-permute-start.12 = (bf16[512,1024]{1,0:T(8,128)(2,1)}, bf16[512,1024]{1,0:T(8,128)(2,1)}, u32[]{:S(2)}, u32[]{:S(2)}) collective-permute-start(bf16[512,1024]{1,0:T(8,128)(2,1)} %get-tuple-element.16), channel_id=1, source_target_pairs={{0,9},{1,8},{2,11},{3,10},{4,13},{5,12},{6,15},{7,14},{8,1},{9,0},... | collective-permute-start | bytes 3145736 | tf_op jit(solution)/shard_map/ppermute | solution.py:221
  17.1 41.2 %collective-permute-start.11 = (bf16[512,1024]{1,0:T(8,128)(2,1)}, bf16[512,1024]{1,0:T(8,128)(2,1)}, u32[]{:S(2)}, u32[]{:S(2)}) collective-permute-start(bf16[512,1024]{1,0:T(8,128)(2,1)} %get-tuple-element.17), channel_id=1, source_target_pairs={{0,8},{1,9},{2,10},{3,11},{4,12},{5,13},{6,14},{7,15},{8,0},{9,1},... | collective-permute-start | bytes 3145736 | tf_op jit(solution)/shard_map/ppermute | solution.py:221
  32.6 30.9 %collective-permute-start.1 = (bf16[512,1024]{1,0:T(8,128)(2,1)}, bf16[512,1024]{1,0:T(8,128)(2,1)}, u32[]{:S(2)}, u32[]{:S(2)}) collective-permute-start(bf16[512,1024]{1,0:T(8,128)(2,1)} %collective-permute-done.two_ref), channel_id=1, source_target_pairs={{0,16},{16,0},{32,48},{48,32},{64,80},{80,64},{96,112},{112,96},{1... | collective-permute-start | bytes 3145736 | tf_op jit(solution)/shard_map/ppermute | solution.py:204
  56.5 7.0 %collective-permute-start.3 = (bf16[512,1024]{1,0:T(8,128)(2,1)}, bf16[512,1024]{1,0:T(8,128)(2,1)}, u32[]{:S(2)}, u32[]{:S(2)}) collective-permute-start(bf16[512,1024]{1,0:T(8,128)(2,1)} %broadcast_select_fusion), channel_id=1, source_target_pairs={{0,16},{16,0},{32,48},{48,32},{64,80},{80,64},{96,112},{112,96},{1... | collective-permute-start | bytes 3145736 | tf_op jit(solution)/shard_map/ppermute | solution.py:204
  56.9 6.7 %copy-start = (bf16[512,512]{1,0:T(8,128)(2,1)S(1)}, bf16[512,512]{1,0:T(8,128)(2,1)}, u32[]{:S(2)}) copy-start(bf16[512,512]{1,0:T(8,128)(2,1)} %keys_ref.3) | copy-start | bytes 1572868
  56.9 6.7 %copy-start.1 = (bf16[512,512]{1,0:T(8,128)(2,1)S(1)}, bf16[512,512]{1,0:T(8,128)(2,1)}, u32[]{:S(2)}) copy-start(bf16[512,512]{1,0:T(8,128)(2,1)} %values_ref.3) | copy-start | bytes 1572868
  56.9 6.7 %copy-start.2 = (bf16[512,512]{1,0:T(8,128)(2,1)S(1)}, bf16[512,512]{1,0:T(8,128)(2,1)}, u32[]{:S(2)}) copy-start(bf16[512,512]{1,0:T(8,128)(2,1)} %q_ref.3) | copy-start | bytes 1572868
  56.9 6.7 %copy-start.3 = (f32[256]{0:T(256)S(1)}, f32[256]{0:T(256)}, u32[]{:S(2)}) copy-start(f32[256]{0:T(256)} %param.14) | copy-start | bytes 3076
  70.3 28.8 %collective-permute-start.13 = (bf16[1536,1024]{1,0:T(8,128)(2,1)S(1)}, bf16[1536,1024]{1,0:T(8,128)(2,1)S(1)}, u32[]{:S(2)}, u32[]{:S(2)}) collective-permute-start(bf16[1536,1024]{1,0:T(8,128)(2,1)S(1)} %constant_dynamic-update-slice_fusion.2.refs_9_), channel_id=1, source_target_pairs={{0,16},{16,0},{32,48},{48,32},{64,80},{80,64},{96,112},{112,96},{1... | collective-permute-start | bytes 9437192 | tf_op jit(solution)/shard_map/ppermute | solution.py:204
  70.4 10.5 %collective-permute-start.4 = (bf16[512,256]{1,0:T(8,128)(2,1)S(1)}, bf16[512,256]{1,0:T(8,128)(2,1)S(1)}, u32[]{:S(2)}, u32[]{:S(2)}) collective-permute-start(bf16[512,256]{1,0:T(8,128)(2,1)S(1)} %shard_map.82.refs_0_), channel_id=1, source_target_pairs={{0,1},{1,0},{2,3},{3,2},{4,5},{5,4},{6,7},{7,6},{8,9},{9,8},{10,11... | collective-permute-start | bytes 786440 | tf_op jit(solution)/shard_map/ppermute | solution.py:210
  70.8 16.2 %collective-permute-start.6 = (bf16[512,256]{1,0:T(8,128)(2,1)S(1)}, bf16[512,256]{1,0:T(8,128)(2,1)S(1)}, u32[]{:S(2)}, u32[]{:S(2)}) collective-permute-start(bf16[512,256]{1,0:T(8,128)(2,1)S(1)} %shard_map.82.refs_0_), channel_id=1, source_target_pairs={{0,9},{1,8},{2,11},{3,10},{4,13},{5,12},{6,15},{7,14},{8,1},{9,0},... | collective-permute-start | bytes 786440 | tf_op jit(solution)/shard_map/ppermute | solution.py:210
  74.2 20.4 %collective-permute-start.5 = (bf16[512,256]{1,0:T(8,128)(2,1)S(1)}, bf16[512,256]{1,0:T(8,128)(2,1)S(1)}, u32[]{:S(2)}, u32[]{:S(2)}) collective-permute-start(bf16[512,256]{1,0:T(8,128)(2,1)S(1)} %shard_map.82.refs_0_), channel_id=1, source_target_pairs={{0,8},{1,9},{2,10},{3,11},{4,12},{5,13},{6,14},{7,15},{8,0},{9,1},... | collective-permute-start | bytes 786440 | tf_op jit(solution)/shard_map/ppermute | solution.py:210
  80.9 13.7 %collective-permute-start.9 = (bf16[512,256]{1,0:T(8,128)(2,1)S(1)}, bf16[512,256]{1,0:T(8,128)(2,1)S(1)}, u32[]{:S(2)}, u32[]{:S(2)}) collective-permute-start(bf16[512,256]{1,0:T(8,128)(2,1)S(1)} %shard_map.83.refs_4_), channel_id=1, source_target_pairs={{0,9},{1,8},{2,11},{3,10},{4,13},{5,12},{6,15},{7,14},{8,1},{9,0},... | collective-permute-start | bytes 786440 | tf_op jit(solution)/shard_map/ppermute | solution.py:210
  82.8 16.4 %collective-permute-start.8 = (bf16[512,256]{1,0:T(8,128)(2,1)S(1)}, bf16[512,256]{1,0:T(8,128)(2,1)S(1)}, u32[]{:S(2)}, u32[]{:S(2)}) collective-permute-start(bf16[512,256]{1,0:T(8,128)(2,1)S(1)} %shard_map.83.refs_4_), channel_id=1, source_target_pairs={{0,8},{1,9},{2,10},{3,11},{4,12},{5,13},{6,14},{7,15},{8,0},{9,1},... | collective-permute-start | bytes 786440 | tf_op jit(solution)/shard_map/ppermute | solution.py:210
  87.0 12.1 %collective-permute-start.7 = (bf16[512,256]{1,0:T(8,128)(2,1)S(1)}, bf16[512,256]{1,0:T(8,128)(2,1)S(1)}, u32[]{:S(2)}, u32[]{:S(2)}) collective-permute-start(bf16[512,256]{1,0:T(8,128)(2,1)S(1)} %shard_map.83.refs_4_), channel_id=1, source_target_pairs={{0,1},{1,0},{2,3},{3,2},{4,5},{5,4},{6,7},{7,6},{8,9},{9,8},{10,11... | collective-permute-start | bytes 786440 | tf_op jit(solution)/shard_map/ppermute | solution.py:210
